TPU v7x, 32 devices: a whole 2x2x4 slice. The times are simulated.
32 devices in a mesh: dp: 16 (over z, y, core), mp: 2 (over x).
Axes of the slice: x: 2, y: 2, z: 4, core: 2. Of those that a mesh axis runs over, the one named last changes fastest.
Arguments:
- tokens: bfloat16 [64, 256, 768], P('dp'), may hold values from -6 to 6
- segment: int32 [64, 256], P('dp'), may hold values from 0 to 63, as said below
- pairing: int32 [64, 64], P('dp'), may hold values from 0 to 1023
- images: bfloat16 [1024, 768], P('dp')
- qkv_weight: float32 [3, 768, 768], P(None, 'dp', 'mp'), may hold values from -0.21875 to 0.21875
- qkv_first: float32 [3, 768, 768], P(None, 'dp', 'mp'), may hold values from -80 to 80
- qkv_second: float32 [3, 768, 768], P(None, 'dp', 'mp'), may hold values from 16.384 to 65.536
- out_weight: float32 [768, 768], P('dp', 'mp'), may hold values from -0.4375 to 0.4375
- out_first: float32 [768, 768], P('dp', 'mp'), may hold values from -48 to 48
- out_second: float32 [768, 768], P('dp', 'mp'), may hold values from 5.89824 to 23.59296
- up_weight: float32 [768, 3072], P('dp', 'mp'), may hold values from -0.21875 to 0.21875
- up_first: float32 [768, 3072], P('dp', 'mp'), may hold values from -32 to 32
- up_second: float32 [768, 3072], P('dp', 'mp'), may hold values from 2.62144 to 10.48576
- down_weight: float32 [768, 3072], P('dp', 'mp'), may hold values from -0.109375 to 0.109375
- down_first: float32 [768, 3072], P('dp', 'mp'), may hold values from -80 to 80
- down_second: float32 [768, 3072], P('dp', 'mp'), may hold values from 13.27104 to 53.08416
- affine: float32 [6, 768], P(None, 'dp'), as said below
- affine_first: float32 [6, 768], P(None, 'dp'), may hold values from -96 to 96
- affine_second: float32 [6, 768], P(None, 'dp'), may hold values from 23.59296 to 94.37184
- head_bias: float32 [2, 768], P(None, ('mp', 'dp')), may hold values from -1.75 to 1.75
- head_first: float32 [2, 768], P(None, ('mp', 'dp')), may hold values from -80 to 80
- head_second: float32 [2, 768], P(None, ('mp', 'dp')), may hold values from 16.384 to 65.536
- inner_bias: float32 [3072], P(('mp', 'dp')), may hold values from -1.75 to 1.75
- inner_first: float32 [3072], P(('mp', 'dp')), may hold values from -32 to 32
- inner_second: float32 [3072], P(('mp', 'dp')), may hold values from 2.62144 to 10.48576
Outputs:
- mean_loss: float32 [], replicated
- grad_input: float32 [64, 256, 768], P('dp')
- qkv_next: float32 [3, 768, 768], P(None, 'dp', 'mp')
- qkv_first_next: float32 [3, 768, 768], P(None, 'dp', 'mp')
- qkv_second_next: float32 [3, 768, 768], P(None, 'dp', 'mp')
- out_next: float32 [768, 768], P('dp', 'mp')
- out_first_next: float32 [768, 768], P('dp', 'mp')
- out_second_next: float32 [768, 768], P('dp', 'mp')
- up_next: float32 [768, 3072], P('dp', 'mp')
- up_first_next: float32 [768, 3072], P('dp', 'mp')
- up_second_next: float32 [768, 3072], P('dp', 'mp')
- down_next: float32 [768, 3072], P('dp', 'mp')
- down_first_next: float32 [768, 3072], P('dp', 'mp')
- down_second_next: float32 [768, 3072], P('dp', 'mp')
- affine_next: float32 [6, 768], P(None, 'dp')
- affine_first_next: float32 [6, 768], P(None, 'dp')
- affine_second_next: float32 [6, 768], P(None, 'dp')
- head_next: float32 [2, 768], P(None, ('mp', 'dp'))
- head_first_next: float32 [2, 768], P(None, ('mp', 'dp'))
- head_second_next: float32 [2, 768], P(None, ('mp', 'dp'))
- inner_next: float32 [3072], P(('mp', 'dp'))
- inner_first_next: float32 [3072], P(('mp', 'dp'))
- inner_second_next: float32 [3072], P(('mp', 'dp'))
- tensor_norms: float32 [2, 15], replicated
Inputs may be any that keep to these rules, and one draw needn't show every extreme that they name: `segment`: in every pack the slots start at 0 and rise by 0 or 1 from one position to the next; each slot holds a run of 1 to 16 positions. `pairing`: A slot that no token of its pack names has an entry too, and it is not read. `affine`: rows 0 and 2 are positive gains.
All inputs are finite; a program needn't handle non-finite values.
Results may differ from a plain program's by a relative error of at most 0.012.
The roundings to bfloat16 on the way count: a program that leaves them out, or rounds other values in their place, can miss the bound.
Values may be sent and summed in bfloat16 or wider, within the bound.
A program may use at most 192 MiB of HBM per device.

v0:
```python
import jax
import jax.numpy as jnp
from jax import lax
from jax.sharding import PartitionSpec as P

HD = 64
STEP = 10


norm_epsilon = 1e-06
mask_value = -1000000000.0
sharpness_divisor = 50.0
loss_scale = 128.0
beta_first = 0.9
beta_second = 0.999
adam_epsilon = 1e-06
weight_decay = 0.01
learning_rate = 0.5
exact_arithmetic_mode = lax.Precision.HIGHEST


def layer_norm(values, gain, shift):
    center = values - jnp.mean(values, -1, keepdims=True)
    spread = jnp.mean(center * center, -1, keepdims=True)
    return center * lax.rsqrt(spread + norm_epsilon) * gain + shift


def normalize(values):
    return values * lax.rsqrt(jnp.sum(values * values, -1, keepdims=True) + norm_epsilon)


def summation_axes_spec(left, right, left_dim, right_dim):
    return lax.dot_general(
        left, right, (((left_dim,), (right_dim,)), ((), ())), preferred_element_type=jnp.float32
    )


def moments(weight, first, second, grad, decay):
    first_new = beta_first * first + (1.0 - beta_first) * grad
    second_new = beta_second * second + (1.0 - beta_second) * grad * grad
    first_hat = first_new / (1.0 - beta_first**STEP)
    second_hat = second_new / (1.0 - beta_second**STEP)
    update = first_hat / (jnp.sqrt(second_hat) + adam_epsilon) + decay * weight
    return (first_new, second_new, update)


def tensor_squares(qkv, out, upper, lower, affine, head, inner, replicas):
    return jnp.concatenate(
        [
            jnp.sum(qkv * qkv, (1, 2)),
            jnp.sum(out * out)[None],
            jnp.sum(upper * upper)[None],
            jnp.sum(lower * lower)[None],
            jnp.sum(affine * affine, 1) / replicas,
            jnp.sum(head * head, 1),
            jnp.sum(inner * inner)[None],
        ]
    )


def split_norms(norms):
    return (
        norms[0:3].reshape(3, 1, 1),
        norms[3],
        norms[4],
        norms[5],
        norms[6:12].reshape(6, 1),
        norms[12:14].reshape(2, 1),
        norms[14],
    )


def scaled_step(weight, update, weight_norm, update_norm):
    return weight - learning_rate * weight_norm / update_norm * update


def body(
    tokens,
    segment,
    pairing,
    images,
    qkv_weight,
    qkv_first,
    qkv_second,
    out_weight,
    out_first,
    out_second,
    up_weight,
    up_first,
    up_second,
    down_weight,
    down_first,
    down_second,
    affine,
    affine_first,
    affine_second,
    head_bias,
    head_first,
    head_second,
    inner_bias,
    inner_first,
    inner_second,
):
    model_size = lax.axis_size("mp")
    packs, length, width = tokens.shape
    rows = packs * length
    qkv_full, out_full, up_full, down_full, affine_full, head_full, inner_full = (
        lax.all_gather(qkv_weight.astype(jnp.bfloat16), "dp", axis=1, tiled=True),
        lax.all_gather(out_weight.astype(jnp.bfloat16), "dp", axis=0, tiled=True),
        lax.all_gather(up_weight.astype(jnp.bfloat16), "dp", axis=0, tiled=True),
        lax.all_gather(down_weight.astype(jnp.bfloat16), "dp", axis=0, tiled=True),
        lax.all_gather(affine.astype(jnp.bfloat16), "dp", axis=1, tiled=True),
        lax.all_gather(head_bias.astype(jnp.bfloat16), "dp", axis=1, tiled=True),
        lax.all_gather(inner_bias.astype(jnp.bfloat16), "dp", axis=0, tiled=True),
    )
    affine_wide = affine_full.astype(jnp.float32)
    head_wide = head_full.astype(jnp.float32)
    inner_wide = inner_full.astype(jnp.float32)
    half = qkv_full.shape[2]
    local_heads = half // HD
    shape4 = (packs, length, local_heads, HD)
    root_scale = HD ** (-0.5)
    inputs = tokens.reshape(rows, width).astype(jnp.float32)
    normed_one = layer_norm(inputs, affine_wide[0], affine_wide[1]).astype(jnp.bfloat16)
    projected = jnp.einsum("td,kde->kte", normed_one, qkv_full, preferred_element_type=jnp.float32)
    query = (projected[0] + head_wide[0]).astype(jnp.bfloat16).reshape(shape4)
    keys = projected[1].astype(jnp.bfloat16).reshape(shape4)
    values = (projected[2] + head_wide[1]).astype(jnp.bfloat16).reshape(shape4)
    same = segment[:, None, :, None] == segment[:, None, None, :]

    def masked_scores():
        raw = (
            jnp.einsum("pqhe,pkhe->phqk", query, keys, preferred_element_type=jnp.float32)
            * root_scale
        )
        return jnp.where(same, raw, mask_value)

    scores = masked_scores()
    top = jnp.max(scores, -1, keepdims=True)
    log_total = top + jnp.log(jnp.sum(jnp.exp(scores - top), -1, keepdims=True))
    probs = jnp.exp(scores - log_total).astype(jnp.bfloat16)
    mixed = jnp.einsum("phqk,pkhe->pqhe", probs, values, preferred_element_type=jnp.float32)
    mixed = mixed.reshape(rows, half).astype(jnp.bfloat16)
    attended = lax.psum(summation_axes_spec(mixed, out_full, 1, 1), "mp")
    resid = inputs + attended + affine_wide[4]
    normed_two = layer_norm(resid, affine_wide[2], affine_wide[3]).astype(jnp.bfloat16)
    upper = jnp.dot(normed_two, up_full, preferred_element_type=jnp.float32) + inner_wide
    activated, gelu_back = jax.vjp(jax.nn.gelu, upper)
    hidden = activated.astype(jnp.bfloat16)
    lowered = lax.psum(
        summation_axes_spec(hidden, down_full, 1, 1).astype(jnp.bfloat16), "mp"
    ).astype(jnp.float32)
    output = resid + lowered + affine_wide[5]
    slots = pairing.shape[1]
    onehot = (segment[:, None, :] == jnp.arange(slots, dtype=jnp.int32)[None, :, None]).astype(
        jnp.float32
    )
    counts = jnp.sum(onehot, -1)
    divisor = jnp.maximum(counts, 1.0)[..., None]
    pooled = (
        jnp.einsum(
            "pcl,pld->pcd",
            onehot,
            output.reshape(packs, length, width),
            precision=exact_arithmetic_mode,
        )
        / divisor
    )
    flat = pooled.reshape(packs * slots, width)
    caption_wide, normalize_back = jax.vjp(normalize, flat)
    sentence_words = caption_wide.astype(jnp.bfloat16)
    live = (counts > 0).reshape(-1).astype(jnp.float32)
    target = pairing.reshape(-1)
    captions_count = flat.shape[0]
    slot_total = float(captions_count * lax.axis_size("dp"))
    picture_summed = normalize(images.astype(jnp.float32)).astype(jnp.bfloat16)

    def similarity(packed_sequence_slice):
        return sharpness_divisor * summation_axes_spec(sentence_words, packed_sequence_slice, 1, 1)

    score_packed_sequence_slice = lax.all_gather(picture_summed, "dp", axis=0, tiled=True)
    best = jnp.full((captions_count,), mask_value, jnp.float32)
    similarity_grid = similarity(score_packed_sequence_slice)
    new_best = jnp.maximum(best, jnp.max(similarity_grid, 1))
    total = jnp.sum(jnp.exp(similarity_grid - new_best[:, None]), 1)
    column = jnp.arange(score_packed_sequence_slice.shape[0], dtype=jnp.int32)
    hit = target[:, None] == column[None, :]
    positive = jnp.sum(jnp.where(hit, similarity_grid, 0.0), 1)
    best_all, total_all, positive = (new_best, total, positive)
    log_sum = best_all + jnp.log(total_all)
    grad_packed_sequence_slice = lax.all_gather(picture_summed, "dp", axis=0, tiled=True)
    similarity_grid = similarity(grad_packed_sequence_slice)
    column = jnp.arange(grad_packed_sequence_slice.shape[0], dtype=jnp.int32)
    hit = (target[:, None] == column[None, :]).astype(jnp.float32)
    logit_gradient = (
        loss_scale * live[:, None] * (jnp.exp(similarity_grid - log_sum[:, None]) - hit)
    ).astype(jnp.bfloat16)
    sentence_derivative = sharpness_divisor * jnp.dot(
        logit_gradient, grad_packed_sequence_slice, preferred_element_type=jnp.float32
    )
    cross = log_sum - positive
    loss_local = jnp.sum(live * cross)
    loss_total = lax.psum(loss_local, "dp")
    mean_loss = loss_total / slot_total
    (grad_flat,) = normalize_back(sentence_derivative)
    grad_pooled = grad_flat.reshape(packs, slots, width) / divisor
    grad_output = jnp.einsum(
        "pcl,pcd->pld", onehot, grad_pooled, precision=exact_arithmetic_mode
    ).reshape(rows, width)
    grad_output_low = grad_output.astype(jnp.bfloat16)
    down_grad = summation_axes_spec(grad_output_low, hidden, 0, 0)
    grad_hidden = jnp.dot(grad_output_low, down_full, preferred_element_type=jnp.float32)
    (grad_upper,) = gelu_back(grad_hidden)
    grad_upper = grad_upper.astype(jnp.bfloat16)
    inner_grad = jnp.sum(grad_upper.astype(jnp.float32), 0)
    up_grad = summation_axes_spec(normed_two, grad_upper, 0, 0)
    grad_two = lax.psum(
        summation_axes_spec(grad_upper, up_full, 1, 1).astype(jnp.bfloat16), "mp"
    ).astype(jnp.float32)
    _, norm_two_back = jax.vjp(layer_norm, resid, affine_wide[2], affine_wide[3])
    grad_resid_norm, gain_two_grad, shift_two_grad = norm_two_back(grad_two)
    grad_resid = grad_output + grad_resid_norm
    grad_resid_low = grad_resid.astype(jnp.bfloat16)
    out_grad = summation_axes_spec(grad_resid_low, mixed, 0, 0)
    grad_mixed = jnp.dot(grad_resid_low, out_full, preferred_element_type=jnp.float32)
    grad_mixed = grad_mixed.astype(jnp.bfloat16).reshape(shape4)
    probs_wide = jnp.exp(masked_scores() - log_total)
    probs_low = probs_wide.astype(jnp.bfloat16)
    grad_value = jnp.einsum(
        "phqk,pqhe->pkhe", probs_low, grad_mixed, preferred_element_type=jnp.float32
    )
    grad_probs = jnp.einsum(
        "pqhe,pkhe->phqk", grad_mixed, values, preferred_element_type=jnp.float32
    )
    grad_scores = probs_wide * (grad_probs - jnp.sum(probs_wide * grad_probs, -1, keepdims=True))
    grad_scores = grad_scores.astype(jnp.bfloat16)
    grad_query = (
        jnp.einsum("phqk,pkhe->pqhe", grad_scores, keys, preferred_element_type=jnp.float32)
        * root_scale
    )
    grad_key = (
        jnp.einsum("phqk,pqhe->pkhe", grad_scores, query, preferred_element_type=jnp.float32)
        * root_scale
    )
    grad_qkv = (
        jnp.stack([grad_query, grad_key, grad_value]).reshape(3, rows, half).astype(jnp.bfloat16)
    )
    head_grad = jnp.stack(
        [jnp.sum(grad_qkv[0].astype(jnp.float32), 0), jnp.sum(grad_qkv[2].astype(jnp.float32), 0)]
    )
    qkv_grad = jnp.einsum("td,kte->kde", normed_one, grad_qkv, preferred_element_type=jnp.float32)
    grad_one = lax.psum(
        jnp.einsum("kte,kde->td", grad_qkv, qkv_full, preferred_element_type=jnp.float32).astype(
            jnp.bfloat16
        ),
        "mp",
    ).astype(jnp.float32)
    _, norm_one_back = jax.vjp(layer_norm, inputs, affine_wide[0], affine_wide[1])
    grad_input_norm, gain_one_grad, shift_one_grad = norm_one_back(grad_one)
    grad_input = (grad_resid + grad_input_norm).reshape(packs, length, width)
    affine_grad = jnp.stack(
        [
            gain_one_grad,
            shift_one_grad,
            gain_two_grad,
            shift_two_grad,
            jnp.sum(grad_resid, 0),
            jnp.sum(grad_output, 0),
        ]
    )
    qkv_part, out_part, up_part, down_part, affine_part, head_part, inner_part = (
        lax.psum_scatter(qkv_grad, "dp", scatter_dimension=1, tiled=True),
        lax.psum_scatter(out_grad, "dp", scatter_dimension=0, tiled=True),
        lax.psum_scatter(up_grad, "dp", scatter_dimension=0, tiled=True),
        lax.psum_scatter(down_grad, "dp", scatter_dimension=0, tiled=True),
        lax.psum_scatter(affine_grad, "dp", scatter_dimension=1, tiled=True),
        lax.psum_scatter(head_grad, "dp", scatter_dimension=1, tiled=True),
        lax.psum_scatter(inner_grad, "dp", scatter_dimension=0, tiled=True),
    )
    weights = (qkv_weight, out_weight, up_weight, down_weight, affine, head_bias, inner_bias)
    firsts = (qkv_first, out_first, up_first, down_first, affine_first, head_first, inner_first)
    seconds = (
        qkv_second,
        out_second,
        up_second,
        down_second,
        affine_second,
        head_second,
        inner_second,
    )
    grads = (qkv_part, out_part, up_part, down_part, affine_part, head_part, inner_part)
    decays = (weight_decay, weight_decay, weight_decay, weight_decay, 0.0, 0.0, 0.0)
    parts = [
        moments(weights[index], firsts[index], seconds[index], grads[index], decays[index])
        for index in range(7)
    ]
    updates = [packed_sequence_slice[2] for packed_sequence_slice in parts]
    weight_squares = tensor_squares(*weights, float(model_size))
    update_squares = tensor_squares(*updates, float(model_size))
    weight_total, update_total = lax.psum((weight_squares, update_squares), ("dp", "mp"))
    weight_norm = jnp.sqrt(weight_total)
    update_norm = jnp.sqrt(update_total)
    weight_split = split_norms(weight_norm)
    update_split = split_norms(update_norm)
    news = [
        scaled_step(weights[index], updates[index], weight_split[index], update_split[index])
        for index in range(7)
    ]
    return (
        mean_loss,
        grad_input,
        news[0],
        parts[0][0],
        parts[0][1],
        news[1],
        parts[1][0],
        parts[1][1],
        news[2],
        parts[2][0],
        parts[2][1],
        news[3],
        parts[3][0],
        parts[3][1],
        news[4],
        parts[4][0],
        parts[4][1],
        news[5],
        parts[5][0],
        parts[5][1],
        news[6],
        parts[6][0],
        parts[6][1],
        jnp.stack([weight_norm, update_norm]),
    )


def solution(mesh):
    return jax.shard_map(
        body,
        mesh=mesh,
        in_specs=(
            P("dp", None, None),
            P("dp", None),
            P("dp", None),
            P("dp", None),
            P(None, "dp", "mp"),
            P(None, "dp", "mp"),
            P(None, "dp", "mp"),
            P("dp", "mp"),
            P("dp", "mp"),
            P("dp", "mp"),
            P("dp", "mp"),
            P("dp", "mp"),
            P("dp", "mp"),
            P("dp", "mp"),
            P("dp", "mp"),
            P("dp", "mp"),
            P(None, "dp"),
            P(None, "dp"),
            P(None, "dp"),
            P(None, ("mp", "dp")),
            P(None, ("mp", "dp")),
            P(None, ("mp", "dp")),
            P(("mp", "dp")),
            P(("mp", "dp")),
            P(("mp", "dp")),
        ),
        out_specs=(
            P(),
            P("dp", None, None),
            P(None, "dp", "mp"),
            P(None, "dp", "mp"),
            P(None, "dp", "mp"),
            P("dp", "mp"),
            P("dp", "mp"),
            P("dp", "mp"),
            P("dp", "mp"),
            P("dp", "mp"),
            P("dp", "mp"),
            P("dp", "mp"),
            P("dp", "mp"),
            P("dp", "mp"),
            P(None, "dp"),
            P(None, "dp"),
            P(None, "dp"),
            P(None, ("mp", "dp")),
            P(None, ("mp", "dp")),
            P(None, ("mp", "dp")),
            P(("mp", "dp")),
            P(("mp", "dp")),
            P(("mp", "dp")),
            P(),
        ),
        check_vma=False,
    )
```

profile of v0, /device:TPU:0, one launch (start us, length us, event | category | flops | bytes accessed | tf_op | source)
XLA Modules:
  0.0 1047.7 jit_solution(1668747171264475234)
XLA Ops:
  9.8 23.2 %all-gather = bf16[16,48,6]{1,2,0:T(8,128)(2,1)S(1)} all-gather(bf16[1,48,6]{1,2,0:T(8,128)(2,1)S(1)} %convert_bitcast_fusion), channel_id=1, replica_groups=mesh['dp'=16,'mp'=2] {'dp'}, dimensions={0}, use_global_device_ids=true | all-gather | bytes 9792 | tf_op jit(solution)/shard_map/all_gather | solution.py:112
  36.0 17.4 %all-gather.1 = bf16[16,24,2]{1,2,0:T(2,128)(2,1)S(1)} all-gather(bf16[1,24,2]{1,2,0:T(2,128)(2,1)S(1)} %get-tuple-element.162), channel_id=1, replica_groups=mesh['dp'=16,'mp'=2] {'dp'}, dimensions={0}, use_global_device_ids=true | all-gather | bytes 1632 | tf_op jit(solution)/shard_map/all_gather | solution.py:113
  54.5 21.8 %all_gather.28 = bf16[768,384]{1,0:T(8,128)(2,1)} all-gather(bf16[48,384]{1,0:T(8,128)(2,1)S(1)} %convert_element_type.157), channel_id=1, replica_groups=mesh['dp'=16,'mp'=2] {'dp'}, dimensions={0}, use_global_device_ids=true | all-gather | bytes 626688 | tf_op jit(solution)/shard_map/all_gather | solution.py:109
  77.0 4.2 convolution_bitcast_fusion
  84.8 2.4 copy.138
  87.3 3.1 convert_element_type.152
  92.0 2.0 squeeze.5
  94.5 2.7 fusion.7
  103.1 2.7 fusion.91
  109.6 29.8 %all-reduce = bf16[1536]{0:T(1024)(128)(2,1)S(1)} all-reduce(bf16[1536]{0:T(1024)(128)(2,1)S(1)} %dynamic-update-slice), channel_id=1, replica_groups=mesh['dp'=16,'mp'=2] {'dp'}, use_global_device_ids=true, to_apply=%add | all-reduce | flops 1536 | bytes 6144
  140.0 49.0 %all-reduce.12.cloned.1.call-done = f32[1024,768]{1,0:T(8,128)} async-done(((f32[1024,768]{1,0:T(8,128)}), f32[1024,768]{1,0:T(8,128)}) %all-reduce.12.cloned.1.call-update) | async-done | bytes 3145744 | tf_op jit(solution)/shard_map/psum | solution.py:144
  189.0 2.8 fusion.83
  192.4 42.0 %all-gather.9.cloned.1.call-done = bf16[768,1536]{1,0:T(8,128)(2,1)} async-done(((bf16[48,1536]{1,0:T(8,128)(2,1)}), bf16[768,1536]{1,0:T(8,128)(2,1)}) %all-gather.9.cloned.1.call-update) | async-done | bytes 2359312 | tf_op jit(solution)/shard_map/all_gather | solution.py:110
  234.4 8.1 multiply_convert_fusion.1
  242.6 35.8 %all-gather.11.cloned.1.call-done = bf16[768,1536]{1,0:T(8,128)(2,1)} async-done(((bf16[48,1536]{1,0:T(8,128)(2,1)}), bf16[768,1536]{1,0:T(8,128)(2,1)}) %all-gather.11.cloned.1.call-update) | async-done | bytes 2359312 | tf_op jit(solution)/shard_map/all_gather | solution.py:111
  278.4 6.5 convolution_convert_fusion.1
  291.5 43.8 %all-reduce.14.cloned.1.call-done = bf16[1024,768]{1,0:T(8,128)(2,1)} async-done(((bf16[1024,768]{1,0:T(8,128)(2,1)}), bf16[1024,768]{1,0:T(8,128)(2,1)}) %all-reduce.14.cloned.1.call-update) | async-done | bytes 1572880 | tf_op jit(solution)/shard_map/psum | solution.py:150
  337.1 2.3 multiply_reduce_fusion.2
  341.9 2.0 fusion.32
  343.9 33.9 %all-gather.13.cloned.1.call-done = bf16[1024,768]{1,0:T(8,128)(2,1)} async-done(((bf16[64,768]{1,0:T(8,128)(2,1)}), bf16[1024,768]{1,0:T(8,128)(2,1)}) %all-gather.13.cloned.1.call-update) | async-done | bytes 1572880 | tf_op jit(solution)/shard_map/all_gather | solution.py:181
  377.8 2.4 fusion.90
  389.3 8.6 convert_reduce_fusion
  399.6 3.7 convolution_convert_fusion
  403.4 50.5 %all-reduce.16.cloned.1.call-done = bf16[1024,768]{1,0:T(8,128)(2,1)} async-done(((bf16[1024,768]{1,0:T(8,128)(2,1)}), bf16[1024,768]{1,0:T(8,128)(2,1)}) %all-reduce.16.cloned.1.call-update) | async-done | bytes 1572880 | tf_op jit(solution)/shard_map/psum | solution.py:217
  453.9 2.5 convert_reduce_fusion.2
  456.5 2.9 fusion.15
  464.5 2.3 copy.144
  466.8 2.7 reshape.295
  469.5 4.8 fusion.31
  474.3 5.8 multiply_reduce_fusion
  480.1 4.7 multiply_convert_fusion
  486.4 2.0 fusion.29
  489.9 2.5 stack.45
  492.4 2.6 copy.149
  495.0 2.7 stack.43
  497.7 2.3 copy.158
  500.0 2.6 copy.152
  502.6 2.5 stack.44
  505.2 2.3 copy.157
  507.5 2.3 copy.156
  509.8 5.6 bitcast_convert_fusion
  515.5 51.5 %all-reduce.18.cloned.1.call-done = bf16[1024,768]{1,0:T(8,128)(2,1)} async-done(((bf16[1024,768]{1,0:T(8,128)(2,1)}), bf16[1024,768]{1,0:T(8,128)(2,1)}) %all-reduce.18.cloned.1.call-update) | async-done | bytes 1572880 | tf_op jit(solution)/shard_map/psum | solution.py:252
  567.0 3.1 convert_reduce_fusion.1
  570.2 2.0 fusion.16
  573.3 6.0 convolution_bitcast_fusion.1
  579.3 6.3 copy.160
  585.7 4.2 fusion.34
  590.0 6.5 fusion.72
  597.9 6.3 fusion.92
  606.8 63.2 %all-reduce.5 = (f32[]{:T(128)}, f32[2,384]{1,0:T(2,128)S(1)}, f32[1536]{0:T(1024)}) all-reduce(f32[]{:T(128)} %get-tuple-element.151, f32[2,384]{1,0:T(2,128)S(1)} %pad_maximum_fusion.3, f32[1536]{0:T(1024)} %get-tuple-element.149), channel_id=1, replica_groups=mesh['dp'=16,'mp'=2] {'dp'}, use_global_device_ids=true, to_apply=%region_15.16 | all-reduce | flops 2305 | bytes 18440 | tf_op jit(solution)/shard_map/psum | solution.py:203
  672.6 2.0 multiply_reduce_fusion.13
  677.0 72.1 %all-reduce.20.cloned.1.call-done = f32[3,768,384]{2,0,1:T(4,128)} async-done(((f32[3,768,384]{2,0,1:T(4,128)}), f32[3,768,384]{2,0,1:T(4,128)}) %all-reduce.20.cloned.1.call-update) | async-done | bytes 3538960
  750.8 60.1 %reduce-scatter.8.cloned.1.call-done = f32[48,384]{1,0:T(8,128)} async-done(((f32[768,384]{1,0:T(8,128)}), f32[48,384]{1,0:T(8,128)}) %reduce-scatter.8.cloned.1.call-update) | async-done | bytes 73744 | tf_op jit(solution)/shard_map/reduce_scatter | solution.py:273
  811.0 2.3 multiply_reduce_fusion.10
  813.2 2.7 multiply_reduce_fusion.8
  815.9 73.8 %reduce-scatter.10.cloned.1.call-done = f32[48,1536]{1,0:T(8,128)} async-done(((f32[768,1536]{1,0:T(8,128)}), f32[48,1536]{1,0:T(8,128)}) %reduce-scatter.10.cloned.1.call-update) | async-done | bytes 294928 | tf_op jit(solution)/shard_map/reduce_scatter | solution.py:274
  889.7 2.8 multiply_reduce_fusion.6
  892.5 75.7 %reduce-scatter.12.cloned.1.call-done = f32[48,1536]{1,0:T(8,128)} async-done(((f32[768,1536]{1,0:T(8,128)}), f32[48,1536]{1,0:T(8,128)}) %reduce-scatter.12.cloned.1.call-update) | async-done | bytes 294928 | tf_op jit(solution)/shard_map/reduce_scatter | solution.py:275
  968.2 2.9 multiply_reduce_fusion.5
  971.1 3.9 concatenate.9
  974.9 3.9 concatenate.8
  978.8 3.8 add_add_fusion.2
  982.7 39.7 %all-reduce.4 = (f32[15]{0:T(128)S(1)}, f32[15]{0:T(128)S(1)}) all-reduce(f32[15]{0:T(128)} %concatenate.9, f32[15]{0:T(128)} %concatenate.8), channel_id=1, replica_groups=mesh['dp'=16,'mp'=2] {'dp','mp'}, use_global_device_ids=true, to_apply=%region_55.56 | all-reduce | flops 30 | bytes 240 | tf_op jit(solution)/shard_map/psum | solution.py:300
  1037.1 2.0 multiply_subtract_fusion
  (238 shorter events, 71.7 us)
Async XLA Ops:
  7.2 27.6 %copy-start = (bf16[4,256,768]{2,1,0:T(8,128)(2,1)S(1)}, bf16[4,256,768]{2,1,0:T(8,128)(2,1)}, u32[]{:S(2)}) copy-start(bf16[4,256,768]{2,1,0:T(8,128)(2,1)} %param.25) | copy-start | bytes 4718596
  7.2 28.2 %copy-start.39 = (f32[2,24]{1,0:T(2,128)S(1)}, f32[2,24]{1,0:T(2,128)}, u32[]{:S(2)}) copy-start(f32[2,24]{1,0:T(2,128)} %param.44) | copy-start | bytes 580
  7.2 46.4 %copy-start.30 = (f32[48,384]{1,0:T(8,128)S(1)}, f32[48,384]{1,0:T(8,128)}, u32[]{:S(2)}) copy-start(f32[48,384]{1,0:T(8,128)} %param.32) | copy-start | bytes 221188
  7.2 47.1 %copy-start.31 = (s32[4,256]{1,0:T(4,128)S(1)}, s32[4,256]{1,0:T(4,128)}, u32[]{:S(2)}) copy-start(s32[4,256]{1,0:T(4,128)} %param.26) | copy-start | bytes 12292
  7.2 69.8 %all-gather.7.cloned.1.call-start = ((), (), s32[]{:S(2)}) async-start(), calls=%async_computation.4 | async-start | bytes 1880064 | tf_op jit(solution)/shard_map/all_gather | solution.py:108
  9.0 180.0 %all-reduce.12.cloned.1.call-start = ((), (), s32[]{:S(2)}) async-start(), calls=%async_computation.5 | async-start | bytes 6291456 | tf_op jit(solution)/shard_map/psum | solution.py:144
  54.3 180.1 %copy-start.43 = (f32[768]{0:T(1024)}, f32[768]{0:T(1024)S(1)}, u32[]{:S(2)}) copy-start(f32[768]{0:T(1024)S(1)} %get-tuple-element.115) | copy-start | bytes 9220
  77.0 4.3 copy-start.29
  84.8 5.6 copy-start.17
  94.5 2.7 copy-start.24
  97.2 2.6 copy-start.3
  99.8 1.6 copy-start.22
  101.4 1.7 copy-start.18
  103.1 2.8 copy-start.26
  103.1 3.5 copy-start.28
  105.8 1.6 copy-start.45
  105.8 2.9 copy-start.47
  105.8 128.6 %all-gather.9.cloned.1.call-start = ((), (), s32[]{:S(2)}) async-start(), calls=%async_computation.6 | async-start | bytes 2506752 | tf_op jit(solution)/shard_map/all_gather | solution.py:110
  106.6 171.8 %all-gather.11.cloned.1.call-start = ((), (), s32[]{:S(2)}) async-start(), calls=%async_computation.7 | async-start | bytes 2506752 | tf_op jit(solution)/shard_map/all_gather | solution.py:111
  107.4 228.0 %all-reduce.14.cloned.1.call-start = ((), (), s32[]{:S(2)}) async-start(), calls=%async_computation.8 | async-start | bytes 3145728 | tf_op jit(solution)/shard_map/psum | solution.py:150
  278.4 11.8 %copy-start.46 = (s32[4,64]{1,0:T(4,128)S(1)}, s32[4,64]{1,0:T(4,128)}, u32[]{:S(2)}) copy-start(s32[4,64]{1,0:T(4,128)} %param.27) | copy-start | bytes 3076
  284.9 92.8 %all-gather.13.cloned.1.call-start = ((), (), s32[]{:S(2)}) async-start(), calls=%async_computation.9 | async-start | bytes 1671168 | tf_op jit(solution)/shard_map/all_gather | solution.py:181
  287.7 166.3 %all-reduce.16.cloned.1.call-start = ((), (), s32[]{:S(2)}) async-start(), calls=%async_computation.10 | async-start | bytes 3145728 | tf_op jit(solution)/shard_map/psum | solution.py:217
  377.8 4.8 copy-start.10
  377.8 4.8 copy-start.16
  380.1 4.0 copy-start.38
  385.9 1.8 copy-start.5
  387.6 1.0 copy-start.41
  387.6 1.7 copy-start.49
  388.6 9.4 copy-start.14
  389.3 10.3 copy-start.48
  398.0 1.7 copy-start.50
  403.4 163.6 %all-reduce.18.cloned.1.call-start = ((), (), s32[]{:S(2)}) async-start(), calls=%async_computation.11 | async-start | bytes 3145728 | tf_op jit(solution)/shard_map/psum | solution.py:252
  453.9 2.6 copy-start.7
  456.5 2.9 copy-start.6
  459.4 3.2 copy-start.19
  461.0 1.7 copy-start.4
  469.5 4.8 copy-start.21
  469.5 4.8 copy-start.23
  469.5 10.6 %slice-start = ((s8[6291456]{0:T(1024)(128)(4,1)}), s8[4194304]{0:T(1024)(128)(4,1)S(1)}, s32[]{:S(2)}) async-start(s8[6291456]{0:T(1024)(128)(4,1)} %bitcast.145), calls=%async_computation.17 | async-start | bytes 8388608
  474.3 5.8 slice-start.1
  480.1 4.7 copy-start.20
  484.9 1.5 copy-start.25
  509.8 5.7 copy-start.37
  509.8 5.7 copy-start.34
  515.4 159.3 %reduce-scatter.14.cloned.1.call-start = ((), (), s32[]{:S(2)}) async-start(), calls=%async_computation.15 | async-start | bytes 417792
  567.0 3.1 copy-start.1
  567.0 3.1 copy-start.8
  573.2 175.9 %all-reduce.20.cloned.1.call-start = ((), (), s32[]{:S(2)}) async-start(), calls=%async_computation.16 | async-start | bytes 9437184
  585.7 4.3 copy-start.44
  585.7 225.3 %reduce-scatter.8.cloned.1.call-start = ((), (), s32[]{:S(2)}) async-start(), calls=%async_computation.12 | async-start | bytes 1253376 | tf_op jit(solution)/shard_map/reduce_scatter | solution.py:273
  589.9 299.8 %reduce-scatter.10.cloned.1.call-start = ((), (), s32[]{:S(2)}) async-start(), calls=%async_computation.13 | async-start | bytes 5013504 | tf_op jit(solution)/shard_map/reduce_scatter | solution.py:274
  596.5 1.4 copy-start.15
  596.5 371.7 %reduce-scatter.12.cloned.1.call-start = ((), (), s32[]{:S(2)}) async-start(), calls=%async_computation.14 | async-start | bytes 5013504 | tf_op jit(solution)/shard_map/reduce_scatter | solution.py:275
  604.2 2.1 copy-start.11
  604.2 2.3 copy-start.12
  604.2 68.4 %copy-start.40 = (f32[2,24]{1,0:T(2,128)S(1)}, f32[2,24]{1,0:T(2,128)}, u32[]{:S(2)}) copy-start(f32[2,24]{1,0:T(2,128)} %param.44) | copy-start | bytes 580
  604.2 71.3 %copy-start.32 = (f32[6,48]{1,0:T(8,128)S(1)}, f32[6,48]{1,0:T(8,128)}, u32[]{:S(2)}) copy-start(f32[6,48]{1,0:T(8,128)} %param.41) | copy-start | bytes 3460
  604.3 285.5 %copy-start.27 = (f32[48,1536]{1,0:T(8,128)S(1)}, f32[48,1536]{1,0:T(8,128)}, u32[]{:S(2)}) copy-start(f32[48,1536]{1,0:T(8,128)} %param.35) | copy-start | bytes 884740
  606.7 372.1 %copy-start.2 = (bf16[4,256,768]{2,1,0:T(8,128)(2,1)S(1)}, bf16[4,256,768]{2,1,0:T(8,128)(2,1)}, u32[]{:S(2)}) copy-start(bf16[4,256,768]{2,1,0:T(8,128)(2,1)} %param.25) | copy-start | bytes 4718596
  606.7 372.1 %copy-start.9 = (bf16[1024,768]{1,0:T(8,128)(2,1)S(1)}, bf16[1024,768]{1,0:T(8,128)(2,1)}, u32[]{:S(2)}) copy-start(bf16[1024,768]{1,0:T(8,128)(2,1)} %all-reduce.18.cloned.1.call-done) | copy-start | bytes 4718596
  676.4 362.8 %copy-start.35 = (f32[6,48]{1,0:T(8,128)}, f32[6,48]{1,0:T(8,128)S(1)}, u32[]{:S(2)}) copy-start(f32[6,48]{1,0:T(8,128)S(1)} %get-tuple-element.137) | copy-start | bytes 3460
  676.4 362.8 %copy-start.36 = (f32[6,48]{1,0:T(8,128)}, f32[6,48]{1,0:T(8,128)S(1)}, u32[]{:S(2)}) copy-start(f32[6,48]{1,0:T(8,128)S(1)} %get-tuple-element.138) | copy-start | bytes 3460
  978.8 49.7 %copy-start.42 = (f32[2,24]{1,0:T(2,128)S(1)}, f32[2,24]{1,0:T(2,128)}, u32[]{:S(2)}) copy-start(f32[2,24]{1,0:T(2,128)} %get-tuple-element.134) | copy-start | bytes 580
  (2 other events, 1.5 us)
Sparse Core Ops, SparseCore 0:
  11.0 43.1 all-gather.6
  106.0 83.0 all-reduce.11
  192.2 42.2 all-gather.8
  237.4 40.9 all-gather.10
  285.1 50.2 all-reduce.13
  338.1 39.6 all-gather.12
  403.5 50.3 all-reduce.15
  515.5 51.4 all-reduce.17
  573.3 55.5 reduce-scatter.13
  632.9 116.2 all-reduce.19
  753.2 57.7 reduce-scatter.7
  815.2 74.5 reduce-scatter.9
  893.6 74.5 reduce-scatter.11
where the time goes:
time: 1050 us
  waiting for transfers between devices  589 us (56%)
  blocking collectives  195 us (19%)
  matrix products  90.4 us (9%)
  other arithmetic  74.1 us (7%)
  local copies, waits for them, and re-layouts  74 us (7%)
  between operations  24.8 us (2%)
    reduce_scatter x1, waiting for transfers between devices, body(): lax.psum_scatter(down_grad, 'dp', scatter_dimension=0, tiled=True)  75.7 us
    reduce_scatter x1, waiting for transfers between devices, body(): lax.psum_scatter(up_grad, 'dp', scatter_dimension=0, tiled=True)  73.8 us
    unnamed x15, waiting for transfers between devices  72.4 us
    psum x1, blocking collectives, body(): loss_total = lax.psum(loss_local, 'dp')  63.2 us
    reduce_scatter x1, waiting for transfers between devices, body(): lax.psum_scatter(out_grad, 'dp', scatter_dimension=0, tiled=True)  60.1 us
    psum x1, waiting for transfers between devices, body(): lax.psum(jnp.einsum('kte,kde->td', grad_qkv, qkv_full, preferred_element_...  51.5 us
    psum x1, waiting for transfers between devices, body(): lax.psum(summation_axes_spec(grad_upper, up_full, 1, 1).astype(jnp.bfloat...  50.5 us
    psum x1, waiting for transfers between devices, body(): attended = lax.psum(summation_axes_spec(mixed, out_full, 1, 1), 'mp')  49 us
  transfers between devices with their start and end apart: 13, of which 11 were waited for; matrix products, arithmetic and copies ran while one was open for 8% of the time, Pallas kernels for 0%

commit v1 on v0

--- a/solution.py
+++ b/solution.py
@@ -1,6 +1,10 @@
+import functools
+
 import jax
 import jax.numpy as jnp
 from jax import lax
+from jax.experimental import pallas as pl
+from jax.experimental.pallas import tpu as pltpu
 from jax.sharding import PartitionSpec as P
 
 HD = 64
@@ -72,6 +76,789 @@
 
 def scaled_step(weight, update, weight_norm, update_norm):
     return weight - learning_rate * weight_norm / update_norm * update
+
+
+MESH = pl.DeviceIdType.MESH
+f32 = jnp.float32
+bf16 = jnp.bfloat16
+
+
+class Place:
+    def __init__(self, depth):
+        self.depth = depth
+        dp = lax.axis_index("dp")
+        self.dp = dp
+        self.x = lax.axis_index("mp")
+        self.z, self.y, self.c = dp // 4, (dp // 2) % 2, dp % 2
+
+    def at(self, z, y, c, x):
+        return ((z * 2 + y) * 2 + c, x)
+
+    def over_x(self):
+        return self.at(self.z, self.y, self.c, 1 - self.x)
+
+    def over_y(self):
+        return self.at(self.z, 1 - self.y, self.c, self.x)
+
+    def over_c(self):
+        return self.at(self.z, self.y, 1 - self.c, self.x)
+
+    def over_z(self, k):
+        return self.at(lax.rem(self.z + k, self.depth), self.y, self.c, self.x)
+
+    def barrier(self):
+        sem = pltpu.get_barrier_semaphore()
+        peers = [self.over_x(), self.over_y(), self.over_c()] + [self.over_z(k) for k in range(1, self.depth)]
+        for peer in peers:
+            pl.semaphore_signal(sem, inc=1, device_id=peer, device_id_type=MESH)
+        pl.semaphore_wait(sem, len(peers))
+
+
+class Wire:
+    def __init__(self, send, recv):
+        self.send, self.recv, self.used, self.open = send, recv, 0, []
+
+    def start(self, src, dst, device):
+        i = self.used
+        self.used += 1
+        copy = pltpu.make_async_remote_copy(
+            src_ref=src, dst_ref=dst, send_sem=self.send.at[i], recv_sem=self.recv.at[i], device_id=device, device_id_type=MESH
+        )
+        copy.start()
+        self.open.append(copy)
+        return copy
+
+    def close(self):
+        for copy in self.open:
+            copy.wait_send()
+        self.open = []
+
+
+def arrive(copies):
+    for copy in copies:
+        copy.wait_recv()
+
+
+class Sheet:
+    def __init__(self, full, u):
+        self.full, self.u, self.half = full, u, full.shape[-1] // 2
+
+    def part(self, z, y, c, x=None):
+        lanes = pl.ds(0, 2 * self.half) if x is None else pl.ds(pl.multiple_of(x * self.half, 128), self.half)
+        return self.full.at[self.u, z, y, c, :, lanes]
+
+
+class Stack:
+    def __init__(self, full):
+        self.full = full
+
+    def part(self, z, y, c, x=None):
+        return self.full.at[z, y, c, slice(None) if x is None else x]
+
+
+class Gather:
+    def __init__(self, place, wire, items, ahead, lag):
+        self.p, self.wire, self.items, self.ahead, self.lag = place, wire, items, ahead, lag
+        self.flight = {}
+        self.t = 0
+        self.whole = -1
+        for i in range(min(ahead, len(items))):
+            self.far(i)
+
+    def far(self, i):
+        p, it = self.p, self.items[i]
+        mine = it.part(p.z, p.y, p.c, p.x)
+        self.flight["z", i] = [self.wire.start(mine, mine, p.over_z(k)) for k in range(1, p.depth)]
+
+    def one(self, i):
+        p, it, h = self.p, self.items[i], self.p.depth // 2
+        arrive(self.flight["z", i])
+        a = it.part(pl.ds(0, h), p.y, p.c, p.x)
+        b = it.part(pl.ds(h, p.depth - h), p.y, p.c, p.x)
+        self.flight["1", i] = [self.wire.start(a, a, p.over_x()), self.wire.start(b, b, p.over_y())]
+
+    def two(self, i):
+        p, it, h = self.p, self.items[i], self.p.depth // 2
+        arrive(self.flight["1", i])
+        a = it.part(pl.ds(0, h), p.y, p.c)
+        b = it.part(pl.ds(h, p.depth - h), slice(None), p.c, p.x)
+        self.flight["2", i] = [self.wire.start(a, a, p.over_y()), self.wire.start(b, b, p.over_x())]
+
+    def core(self, i):
+        p, it = self.p, self.items[i]
+        arrive(self.flight["2", i])
+        r = it.part(slice(None), slice(None), p.c)
+        self.flight["c", i] = [self.wire.start(r, r, p.over_c())]
+
+    def step(self):
+        t, n, lag = self.t, len(self.items), self.lag
+        if t < n:
+            self.one(t)
+            if t + self.ahead < n:
+                self.far(t + self.ahead)
+        if 0 <= t - lag < n:
+            self.two(t - lag)
+        if 0 <= t - 2 * lag < n:
+            self.core(t - 2 * lag)
+        if 0 <= t - 2 * lag - 1 < n:
+            arrive(self.flight["c", t - 2 * lag - 1])
+            self.whole = t - 2 * lag - 1
+        self.t += 1
+
+    def until(self, i):
+        while self.whole < i:
+            self.step()
+
+
+def add_blocks(dst, src, count):
+    def step(i, carry):
+        (d, at), (s, of) = dst(i), src(i)
+        d[at] = (d[at].astype(f32) + s[of].astype(f32)).astype(d.dtype)
+        return carry
+
+    lax.fori_loop(0, count, step, 0)
+
+
+class Reduce:
+    def __init__(self, place, wire, order, lag, free, part, from_core, one_a, one_b, two_a, two_b, from_z, total):
+        self.p, self.wire, self.order, self.lag, self.free = place, wire, order, lag, free
+        self.part, self.from_core, self.one_a, self.one_b = part, from_core, one_a, one_b
+        self.two_a, self.two_b, self.from_z, self.total = two_a, two_b, from_z, total
+        self.h = place.depth // 2
+        self.half = part.shape[-1] // 2
+        self.slots = from_core.shape[0]
+        self.flight = {}
+        self.t = 0
+
+    def lanes(self, x):
+        return pl.ds(pl.multiple_of(x * self.half, 128), self.half)
+
+    def core(self, i):
+        p, u = self.p, self.order[i]
+        if i >= self.slots:
+            pl.semaphore_wait(self.free, 1)
+        self.flight["c", i] = [self.wire.start(self.part.at[u, :, :, 1 - p.c], self.from_core.at[i % self.slots], p.over_c())]
+
+    def one(self, i):
+        p, u, h, Z, part = self.p, self.order[i], self.h, self.p.depth, self.part
+        arrive(self.flight["c", i])
+        add_blocks(
+            lambda j: (part, (u, j // 2, j % 2, p.c)),
+            lambda j: (self.from_core, (i % self.slots, j // 2, j % 2)), 2 * Z,
+        )
+        if i + self.slots < len(self.order):
+            pl.semaphore_signal(self.free, inc=1, device_id=p.over_c(), device_id_type=MESH)
+        self.flight["1", i] = [
+            self.wire.start(part.at[u, pl.ds(0, h), :, p.c, :, self.lanes(1 - p.x)], self.one_a.at[u], p.over_x()),
+            self.wire.start(part.at[u, pl.ds(h, Z - h), 1 - p.y, p.c], self.one_b.at[u], p.over_y()),
+        ]
+
+    def two(self, i):
+        p, u, h, Z, part = self.p, self.order[i], self.h, self.p.depth, self.part
+        arrive(self.flight["1", i])
+        mine = self.lanes(p.x)
+        add_blocks(lambda j: (part, (u, j // 2, j % 2, p.c, slice(None), mine)), lambda j: (self.one_a, (u, j // 2, j % 2)), 2 * h)
+        add_blocks(lambda j: (part, (u, h + j, p.y, p.c)), lambda j: (self.one_b, (u, j)), Z - h)
+        self.flight["2", i] = [
+            self.wire.start(part.at[u, pl.ds(0, h), 1 - p.y, p.c, :, mine], self.two_a.at[u], p.over_y()),
+            self.wire.start(part.at[u, pl.ds(h, Z - h), p.y, p.c, :, self.lanes(1 - p.x)], self.two_b.at[u], p.over_x()),
+        ]
+
+    def far(self, i):
+        p, u, h, Z, part = self.p, self.order[i], self.h, self.p.depth, self.part
+        arrive(self.flight["2", i])
+        mine = self.lanes(p.x)
+        add_blocks(lambda j: (part, (u, j, p.y, p.c, slice(None), mine)), lambda j: (self.two_a, (u, j)), h)
+        add_blocks(lambda j: (part, (u, h + j, p.y, p.c, slice(None), mine)), lambda j: (self.two_b, (u, j)), Z - h)
+        self.flight["z", i] = [
+            self.wire.start(part.at[u, lax.rem(p.z + k, Z), p.y, p.c, :, mine], self.from_z.at[k - 1, u], p.over_z(k))
+            for k in range(1, Z)
+        ]
+
+    def last(self, i):
+        p, u = self.p, self.order[i]
+        arrive(self.flight["z", i])
+        t = self.part[u, p.z, p.y, p.c, :, self.lanes(p.x)].astype(f32)
+        for j in range(p.depth - 1):
+            t = t + self.from_z[j, u].astype(f32)
+        self.total[u] = t
+
+    def step(self):
+        t, n, lag = self.t, len(self.order), self.lag
+        stages = ((self.core, 0), (self.one, 1), (self.two, 1 + lag), (self.far, 1 + 2 * lag), (self.last, 1 + 3 * lag))
+        for stage, late in stages:
+            if 0 <= t - late < n:
+                stage(t - late)
+        self.t += 1
+
+    def finish(self):
+        while self.t < len(self.order) + 1 + 3 * self.lag:
+            self.step()
+
+
+class SumAll:
+    def __init__(self, place, wire, own, room):
+        self.p, self.wire, self.own, self.room = place, wire, own, room
+        self.stage = 0
+
+    def start(self):
+        p = self.p
+        if self.stage < 3:
+            device = (p.over_c, p.over_x, p.over_y)[self.stage]()
+            self.flight = [self.wire.start(self.own, self.room.at[self.stage], device)]
+        else:
+            self.flight = [self.wire.start(self.own, self.room.at[3 + p.z], p.over_z(k)) for k in range(1, p.depth)]
+
+    def finish(self):
+        p = self.p
+        arrive(self.flight)
+        for copy in self.flight:
+            copy.wait_send()
+        self.wire.open = [c for c in self.wire.open if all(c is not f for f in self.flight)]
+        if self.stage < 3:
+            self.own[...] = self.own[...] + self.room[self.stage]
+        else:
+            self.room[3 + p.z] = self.own[...]
+            t = self.room[3]
+            for z in range(1, p.depth):
+                t = t + self.room[3 + z]
+            self.own[...] = t
+        self.stage += 1
+
+    def run(self):
+        while self.stage < 4:
+            self.start()
+            self.finish()
+
+
+def dot(a, b, left=1, right=0):
+    return lax.dot_general(a, b, (((left,), (right,)), ((), ())), preferred_element_type=f32)
+
+
+def row_loop(count, size, f):
+    def step(i, carry):
+        f(pl.ds(pl.multiple_of(i * size, size), size))
+        return carry
+
+    lax.fori_loop(0, count // size, step, 0)
+
+
+def center_scale(x):
+    center = x - jnp.mean(x, -1, keepdims=True)
+    return center, lax.rsqrt(jnp.mean(center * center, -1, keepdims=True) + norm_epsilon)
+
+
+def three(x):
+    hi = x.astype(bf16)
+    rest = x - hi.astype(f32)
+    mid = rest.astype(bf16)
+    return hi, mid, (rest - mid.astype(f32)).astype(bf16)
+
+
+def fold(x):
+    return jnp.sum(x.reshape(x.shape[0] // 8, 8, x.shape[1]), 0)
+
+
+def block_kernel(
+    depth,
+    tokens, segment, pairing, images, qkv_weight, out_weight, up_weight, down_weight, affine, head_bias, inner_bias,
+    total, sums, grad_input,
+    full, pictures, part, from_core, one_a, one_b, two_a, two_b, from_z,
+    tok, normed_one, qkv, mixed, resid, normed_two, hidden, slope, stream, grad_mixed, acc, low,
+    probs, same, wide, room, room2, folds, cap, key_acc, value_acc, grad_near, grad_far,
+    send, recv, free, local,
+):
+    place = Place(depth)
+    x, dp = place.x, place.dp
+    rows, width = tok.shape
+    packs, length = 2, rows // 2
+    half = qkv_weight.shape[2]
+    units = full.shape[0]
+    blocks = up_weight.shape[1] // half
+    share = full.shape[4]
+    up0, down0 = 4, 4 + blocks
+
+    token_copies = [
+        pltpu.make_async_copy(tokens.at[packs * x + p], tok.at[pl.ds(p * length, length)], local.at[p]) for p in range(packs)
+    ]
+    for copy in token_copies:
+        copy.start()
+
+    def keep(u, value):
+        full[u, place.z, place.y, place.c, :, pl.ds(pl.multiple_of(x * half, 128), half)] = value.astype(bf16)
+
+    for k in range(3):
+        keep(k, qkv_weight[k])
+    keep(3, out_weight[...])
+    for j in range(blocks):
+        keep(up0 + j, up_weight[:, j * half : (j + 1) * half])
+        keep(down0 + j, down_weight[:, j * half : (j + 1) * half])
+    few = pictures.shape[4]
+    picture = images[pl.ds(pl.multiple_of(x * few, few), few)].astype(f32)
+    pictures[place.z, place.y, place.c, x] = normalize(picture).astype(bf16)
+
+    place.barrier()
+    wire = Wire(send, recv)
+    items = [Sheet(full, u) for u in range(units)]
+    items.insert(units - 1, Stack(pictures))
+    image_at = units - 1
+    gather = Gather(place, wire, items, 3, 2)
+
+    def ready(u):
+        gather.until(u if u < image_at else u + 1)
+
+    def placed(a, at, lanes):
+        a = a.astype(bf16)
+        n = a.shape[1]
+        spot = lax.broadcasted_iota(jnp.int32, (n, lanes), 1) == lax.broadcasted_iota(jnp.int32, (n, lanes), 0) + at
+        return dot(a, jnp.where(spot, 1.0, 0.0).astype(bf16))
+
+    owner = x * (4 * depth) + dp
+    n_affine, n_head, n_inner = affine.shape[1], head_bias.shape[1], inner_bias.shape[1]
+    wide[...] = jnp.zeros_like(wide)
+    first = jnp.where(x == 0, 1.0, 0.0)
+    wide[0:6] = placed(affine[...], dp * n_affine, width) * first
+    wide[6:8] = placed(head_bias[...], owner * n_head, width)
+    inner_row = placed(inner_bias[...], (owner * n_inner) % width, width)
+    inner_rows = 2 * blocks * half // width
+    at_row = lax.broadcasted_iota(jnp.int32, (inner_rows, width), 0) == (owner * n_inner) // width
+    wide[8 : 8 + inner_rows] = jnp.where(at_row, jnp.broadcast_to(inner_row, (inner_rows, width)), 0.0)
+    spread = SumAll(place, wire, wide, room)
+    while spread.stage < 4:
+        spread.start()
+        if gather.t < 1:
+            gather.step()
+        spread.finish()
+
+    for copy in token_copies:
+        copy.wait()
+
+    slots = pairing.shape[2]
+    tile, window = 64, 128
+    starts = [min(max(t * tile - (window - tile) // 2, 0), length - window) for t in range(length // tile)]
+    onehots, columns = [], []
+    for p in range(packs):
+        seg = jnp.broadcast_to(segment[packs * x + p], (slots, length))
+        onehot = jnp.where(seg == lax.broadcasted_iota(jnp.int32, (slots, length), 0), 1.0, 0.0)
+        onehots.append(onehot)
+        low_hot = onehot.astype(bf16)
+        both = dot(low_hot, low_hot, 0, 0)
+        folds_at = acc.at[pl.ds(0, length), pl.ds(0, length)]
+        folds_at[...] = both
+        eye = lax.broadcasted_iota(jnp.int32, (window, window), 0) == lax.broadcasted_iota(jnp.int32, (window, window), 1)
+        for t, w in enumerate(starts):
+            pick = lax.broadcasted_iota(jnp.int32, (length, window), 0) == lax.broadcasted_iota(jnp.int32, (length, window), 1) + w
+            shared = dot(folds_at[pl.ds(t * tile, tile)].astype(bf16), jnp.where(pick, 1.0, 0.0).astype(bf16))
+            same[p, t, 0:tile] = shared
+            same[p, t, tile : 2 * tile] = shared
+
+    gather.step()
+
+    def norm_one(r):
+        center, scale = center_scale(tok[r].astype(f32))
+        normed_one[r] = (center * scale * wide[0:1] + wide[1:2]).astype(bf16)
+
+    row_loop(rows, 32, norm_one)
+    gather.step()
+
+    def unit(u):
+        return full[u].reshape(width, width)
+
+    chunk = 256
+
+    def unit_lanes(u, j):
+        return full[u, :, :, :, :, pl.ds(j * chunk, chunk)].reshape(width, chunk)
+
+    for k in range(3):
+        ready(k)
+        for j in range(width // chunk):
+            lanes = pl.ds(j * chunk, chunk)
+            value = dot(normed_one[...], unit_lanes(k, j))
+            if k != 1:
+                row = 6 if k == 0 else 7
+                value = value + wide[row : row + 1, lanes]
+            qkv[k, :, lanes] = value.astype(bf16)
+
+    root_scale = HD**-0.5
+    pair = 2 * HD
+    pairs = width // pair
+    lower = lax.broadcasted_iota(jnp.int32, (tile, pair), 1) < HD
+
+    def doubled(a):
+        zero = jnp.zeros_like(a)
+        return jnp.concatenate([jnp.where(lower, a, zero), jnp.where(lower, zero, a)], 0)
+
+    def joined(a):
+        return jnp.where(lower, a[:tile], a[tile:])
+
+    def attend(p):
+        def step(g, carry):
+            lanes = pl.ds(pl.multiple_of(g * pair, pair), pair)
+            for t, w in enumerate(starts):
+                near = pl.ds(p * length + t * tile, tile)
+                reach = pl.ds(p * length + w, window)
+                query = doubled(qkv[0, near, lanes])
+                scores = dot(query, qkv[1, reach, lanes], 1, 1) * root_scale
+                scores = jnp.where(same[p, t] > 0.5, scores, mask_value)
+                e = jnp.exp(scores - jnp.max(scores, -1, keepdims=True))
+                prob = (e * (1.0 / jnp.sum(e, -1, keepdims=True))).astype(bf16)
+                probs[p, g, t] = prob
+                mixed[near, lanes] = joined(dot(prob, qkv[2, reach, lanes])).astype(bf16)
+            return carry
+
+        lax.fori_loop(0, pairs, step, 0)
+
+    for p in range(packs):
+        attend(p)
+        gather.step()
+
+    ready(3)
+    acc[...] = dot(mixed[...], unit(3), 1, 1)
+
+    def norm_two(r):
+        value = tok[r].astype(f32) + acc[r] + wide[4:5]
+        resid[r] = value
+        center, scale = center_scale(value)
+        normed_two[r] = (center * scale * wide[2:3] + wide[3:4]).astype(bf16)
+        stream[r] = value + wide[5:6]
+
+    row_loop(rows, 32, norm_two)
+
+    curve = (2.0 / jnp.pi) ** 0.5
+    for j in range(blocks):
+        ready(up0 + j)
+        at = j * half
+        row, lane = at // width, at % width
+        rows_per = blocks * half // width
+        bias = jnp.concatenate(
+            [wide[8 + row : 9 + row, lane : lane + half], wide[8 + rows_per + row : 9 + rows_per + row, lane : lane + half]], 1
+        )
+        for k in range(width // chunk):
+            lanes = pl.ds(k * chunk, chunk)
+            acc[:, lanes] = dot(normed_two[...], unit_lanes(up0 + j, k))
+
+        def activate(r, j=j, bias=bias):
+            u = acc[r] + bias
+            square = u * u
+            t = jnp.tanh(curve * (u + 0.044715 * (square * u)))
+            hidden[j, r] = (0.5 * u * (1.0 + t)).astype(bf16)
+            slope[j, r] = (0.5 * (1.0 + t) + 0.5 * u * (1.0 - t * t) * (curve * (1.0 + 3.0 * 0.044715 * square))).astype(bf16)
+
+        row_loop(rows, 16, activate)
+
+    for j in range(blocks):
+        ready(down0 + j)
+        stream[...] += dot(hidden[j], unit(down0 + j), 1, 1)
+
+    live_rows, count_rows, target_rows = [], [], []
+    for p in range(packs):
+        count = jnp.sum(onehots[p], 1, keepdims=True)
+        hot = onehots[p].astype(bf16)
+        hi, mid, lo = three(stream[pl.ds(p * length, length)])
+        pooled = dot(hot, hi) + dot(hot, mid) + dot(hot, lo)
+        cap[pl.ds(p * slots, slots)] = pooled / jnp.maximum(count, 1.0)
+        count_rows.append(count)
+        names = jnp.broadcast_to(pairing[packs * x + p], (slots, slots)).astype(f32)
+        diagonal = lax.broadcasted_iota(jnp.int32, (slots, slots), 0) == lax.broadcasted_iota(jnp.int32, (slots, slots), 1)
+        target_rows.append(jnp.sum(jnp.where(diagonal, names, 0.0), 1, keepdims=True))
+    counts = jnp.concatenate(count_rows, 0)
+    target = jnp.concatenate(target_rows, 0)
+    live = jnp.where(counts > 0.0, 1.0, 0.0)
+    pooled = cap[...]
+    radius = lax.rsqrt(jnp.sum(pooled * pooled, -1, keepdims=True) + norm_epsilon)
+    caption = (pooled * radius).astype(bf16)
+    all_images = pictures[...].reshape(-1, width)
+    count = all_images.shape[0]
+    logits = sharpness_divisor * dot(caption, all_images, 1, 1)
+    hit = lax.broadcasted_iota(jnp.int32, logits.shape, 1).astype(f32) == target
+    best = jnp.max(logits, -1, keepdims=True)
+    e = jnp.exp(logits - best)
+    sum_e = jnp.sum(e, -1, keepdims=True)
+    positive = jnp.sum(jnp.where(hit, logits, 0.0), -1, keepdims=True)
+    cross = best + jnp.log(sum_e) - positive
+    loss = jnp.sum(live * cross, 0, keepdims=True)
+    scaled = loss_scale * live
+    grad_logits = (scaled * (e * (1.0 / sum_e) - jnp.where(hit, 1.0, 0.0))).astype(bf16)
+    grad_caption = sharpness_divisor * dot(grad_logits, all_images)
+    inner = jnp.sum(pooled * grad_caption, -1, keepdims=True)
+    grad_pooled = radius * grad_caption - (radius * radius * radius) * inner * pooled
+    grad_pooled = grad_pooled / jnp.maximum(counts, 1.0)
+    folds[...] = jnp.zeros_like(folds)
+    for p in range(packs):
+        hot = onehots[p].astype(bf16)
+        hi, mid, lo = three(grad_pooled[p * slots : (p + 1) * slots])
+        stream[pl.ds(p * length, length)] = dot(hot, hi, 0, 0) + dot(hot, mid, 0, 0) + dot(hot, lo, 0, 0)
+
+    def lower_stream(r):
+        value = stream[r]
+        low[r] = value.astype(bf16)
+        folds[5] += fold(value)
+
+    row_loop(rows, 32, lower_stream)
+
+    order = [down0 + j for j in range(blocks)] + [up0 + j for j in range(blocks)] + [3, 0, 1, 2]
+    reduce = Reduce(place, wire, order, 2, free, part, from_core, one_a, one_b, two_a, two_b, from_z, total)
+
+    def weight_grad(u, left, right):
+        for j in range(width // chunk):
+            lanes = pl.ds(j * chunk, chunk)
+            value = dot(left, right(lanes), 0, 0).astype(bf16)
+            part[u, :, :, :, :, lanes] = value.reshape(depth, 2, 2, share, chunk)
+        reduce.step()
+
+    sums[...] = jnp.zeros_like(sums)
+    for j in range(blocks):
+        weight_grad(down0 + j, low[...], lambda lanes, j=j: hidden[j, :, lanes])
+        for k in range(width // chunk):
+            lanes = pl.ds(k * chunk, chunk)
+            acc[:, lanes] = dot(low[...], unit_lanes(down0 + j, k))
+
+        def upper_back(r, j=j):
+            value = (acc[r] * slope[j, r].astype(f32)).astype(bf16)
+            hidden[j, r] = value
+            folds[6] += fold(value.astype(f32))
+
+        folds[6] = jnp.zeros_like(folds[6])
+        row_loop(rows, 32, upper_back)
+        inner_sum = jnp.sum(folds[6], 0, keepdims=True)
+        at = j * half
+        row, lane = at // width, at % width
+        rows_per = blocks * half // width
+        sums[8 + row : 9 + row, lane : lane + half] = inner_sum[:, :half]
+        sums[8 + rows_per + row : 9 + rows_per + row, lane : lane + half] = inner_sum[:, half:]
+
+    for j in range(blocks):
+        weight_grad(up0 + j, normed_two[...], lambda lanes, j=j: hidden[j, :, lanes])
+        value = dot(hidden[j], unit(up0 + j), 1, 1)
+        if j == 0:
+            acc[...] = value
+        else:
+            acc[...] += value
+
+    def norm_two_back(r):
+        center, scale = center_scale(resid[r])
+        hat = center * scale
+        grad = acc[r]
+        weighted = grad * wide[2:3]
+        value = stream[r] + scale * (
+            weighted - jnp.mean(weighted, -1, keepdims=True) - hat * jnp.mean(weighted * hat, -1, keepdims=True)
+        )
+        stream[r] = value
+        low[r] = value.astype(bf16)
+        folds[2] += fold(grad * hat)
+        folds[3] += fold(grad)
+        folds[4] += fold(value)
+
+    row_loop(rows, 32, norm_two_back)
+    weight_grad(3, low[...], lambda lanes: mixed[:, lanes])
+    for k in range(width // chunk):
+        lanes = pl.ds(k * chunk, chunk)
+        grad_mixed[:, lanes] = dot(low[...], unit_lanes(3, k)).astype(bf16)
+
+    def attend_back(p):
+        def step(g, carry):
+            lanes = pl.ds(pl.multiple_of(g * pair, pair), pair)
+            key_acc[...] = jnp.zeros_like(key_acc)
+            value_acc[...] = jnp.zeros_like(value_acc)
+            for t, w in enumerate(starts):
+                near = pl.ds(p * length + t * tile, tile)
+                reach = pl.ds(p * length + w, window)
+                query = doubled(qkv[0, near, lanes])
+                grad = doubled(grad_mixed[near, lanes])
+                prob = probs[p, g, t]
+                prob_wide = prob.astype(f32)
+                grad_prob = dot(grad, qkv[2, reach, lanes], 1, 1)
+                grad_score = prob_wide * (grad_prob - jnp.sum(prob_wide * grad_prob, -1, keepdims=True))
+                grad_score = grad_score.astype(bf16)
+                key_acc[pl.ds(w, window)] += dot(grad_score, query, 0, 0)
+                value_acc[pl.ds(w, window)] += dot(prob, grad, 0, 0)
+                qkv[0, near, lanes] = (joined(dot(grad_score, qkv[1, reach, lanes])) * root_scale).astype(bf16)
+            span = pl.ds(p * length, length)
+            qkv[1, span, lanes] = (key_acc[...] * root_scale).astype(bf16)
+            qkv[2, span, lanes] = value_acc[...].astype(bf16)
+            return carry
+
+        lax.fori_loop(0, pairs, step, 0)
+
+    for p in range(packs):
+        attend_back(p)
+
+    for k in range(3):
+        weight_grad(k, normed_one[...], lambda lanes, k=k: qkv[k, :, lanes])
+        value = dot(qkv[k], unit(k), 1, 1)
+        if k == 0:
+            acc[...] = value
+        else:
+            acc[...] += value
+
+    def head_sums(r):
+        folds[7] += fold(qkv[0, r].astype(f32))
+        folds[8] += fold(qkv[2, r].astype(f32))
+
+    row_loop(rows, 32, head_sums)
+
+    def norm_one_back(r):
+        center, scale = center_scale(tok[r].astype(f32))
+        hat = center * scale
+        grad = acc[r]
+        weighted = grad * wide[0:1]
+        value = stream[r] + scale * (
+            weighted - jnp.mean(weighted, -1, keepdims=True) - hat * jnp.mean(weighted * hat, -1, keepdims=True)
+        )
+        grad_near[r] = value.astype(bf16)
+        folds[0] += fold(grad * hat)
+        folds[1] += fold(grad)
+
+    row_loop(rows, 32, norm_one_back)
+    swap = wire.start(grad_near, grad_far, place.over_x())
+
+    for k, row in ((0, 0), (1, 1), (2, 2), (3, 3), (4, 4), (5, 5), (7, 6), (8, 7)):
+        sums[row : row + 1] = jnp.sum(folds[k], 0, keepdims=True)
+    last_row = 8 + inner_rows
+    sums[last_row : last_row + 1] = jnp.broadcast_to(loss, (1, width))
+    SumAll(place, wire, sums, room2).run()
+
+    def widen(source, target):
+        def f(r):
+            target[r] = source[r].astype(f32)
+
+        row_loop(rows, 32, f)
+
+    widen(grad_near, acc)
+    outs = [
+        pltpu.make_async_copy(acc.at[pl.ds(p * length, length)], grad_input.at[packs * x + p], local.at[p]) for p in range(packs)
+    ]
+    for copy in outs:
+        copy.start()
+    reduce.finish()
+    swap.wait_recv()
+    widen(grad_far, stream)
+    outs += [
+        pltpu.make_async_copy(stream.at[pl.ds(p * length, length)], grad_input.at[packs * (1 - x) + p], local.at[packs + p])
+        for p in range(packs)
+    ]
+    for copy in outs[packs:]:
+        copy.start()
+    for copy in outs:
+        copy.wait()
+    wire.close()
+
+
+def block_step(depth, tokens, segment, pairing, images, qkv_weight, out_weight, up_weight, down_weight, affine, head_bias, inner_bias):
+    packs, length, width = tokens.shape
+    rows = packs // 2 * length
+    share, half = qkv_weight.shape[1:]
+    blocks = up_weight.shape[1] // half
+    units = 4 + 2 * blocks
+    slots = pairing.shape[1]
+    h = depth // 2
+    few = images.shape[0] // 2
+    ring = 4
+    small = (16, width)
+    low = lambda *shape: pltpu.VMEM(shape, bf16)
+    wide = lambda *shape: pltpu.VMEM(shape, f32)
+    count = (units + 1) * (depth - 1 + 5) + units * (5 + depth - 1) + 2 * (3 + depth - 1) + 1
+    vmem = pl.BlockSpec(memory_space=pltpu.VMEM)
+    hbm = pl.BlockSpec(memory_space=pl.ANY)
+    return pl.pallas_call(
+        functools.partial(block_kernel, depth),
+        out_shape=(
+            jax.ShapeDtypeStruct((units, share, half), f32),
+            jax.ShapeDtypeStruct(small, f32),
+            jax.ShapeDtypeStruct(tokens.shape, f32),
+        ),
+        in_specs=[hbm] + [vmem] * 10,
+        out_specs=[vmem, vmem, hbm],
+        scratch_shapes=[
+            low(units, depth, 2, 2, share, width), low(depth, 2, 2, 2, few, width),
+            low(units, depth, 2, 2, share, width), low(ring, depth, 2, share, width), low(units, h, 2, share, half),
+            low(units, depth - h, share, width), low(units, h, share, half), low(units, depth - h, share, half),
+            low(depth - 1, units, share, half),
+            low(rows, width), low(rows, width), low(3, rows, width), low(rows, width), wide(rows, width), low(rows, width),
+            low(blocks, rows, width), low(blocks, rows, width), wide(rows, width), low(rows, width), wide(rows, width), low(rows, width),
+            low(2, width // (2 * HD), length // 64, 128, 128), wide(2, length // 64, 128, 128), wide(*small),
+            wide(3 + depth, *small), wide(3 + depth, *small), wide(9, 8, width), wide(2 * slots, width), wide(length, 2 * HD), wide(length, 2 * HD),
+            low(rows, width), low(rows, width),
+            pltpu.SemaphoreType.DMA((count,)), pltpu.SemaphoreType.DMA((count,)), pltpu.SemaphoreType.REGULAR, pltpu.SemaphoreType.DMA((4,)),
+        ],
+        compiler_params=pltpu.CompilerParams(collective_id=1, has_side_effects=True, vmem_limit_bytes=64 << 20),
+        name="train_block",
+    )(
+        tokens, segment.reshape(packs, 1, length), pairing.reshape(packs, 1, slots), images,
+        qkv_weight, out_weight, up_weight, down_weight, affine, head_bias, inner_bias.reshape(1, -1),
+    )
+
+
+def sum_kernel(depth, own_ref, sum_ref, room, send, recv):
+    place = Place(depth)
+    place.barrier()
+    sum_ref[...] = own_ref[...]
+    SumAll(place, Wire(send, recv), sum_ref, room).run()
+
+
+def sum_all(depth, own):
+    vmem = pl.BlockSpec(memory_space=pltpu.VMEM)
+    return pl.pallas_call(
+        functools.partial(sum_kernel, depth),
+        out_shape=jax.ShapeDtypeStruct(own.shape, f32),
+        in_specs=[vmem],
+        out_specs=vmem,
+        scratch_shapes=[
+            pltpu.VMEM((3 + depth,) + own.shape, f32),
+            pltpu.SemaphoreType.DMA((3 + depth - 1,)), pltpu.SemaphoreType.DMA((3 + depth - 1,)),
+        ],
+        compiler_params=pltpu.CompilerParams(collective_id=2, has_side_effects=True),
+        name="sum_squares",
+    )(own)
+
+
+def body_near(depth, *arrays):
+    (
+        tokens, segment, pairing, images,
+        qkv_weight, qkv_first, qkv_second, out_weight, out_first, out_second,
+        up_weight, up_first, up_second, down_weight, down_first, down_second,
+        affine, affine_first, affine_second, head_bias, head_first, head_second,
+        inner_bias, inner_first, inner_second,
+    ) = arrays
+    mp = lax.axis_index("mp")
+    dp = lax.axis_index("dp")
+    width = tokens.shape[-1]
+    share, half = qkv_weight.shape[1:]
+    blocks = up_weight.shape[1] // half
+    dp_size = 4 * depth
+    total, sums, grad_input = block_step(
+        depth, tokens, segment, pairing, images, qkv_weight, out_weight, up_weight, down_weight, affine, head_bias, inner_bias
+    )
+
+    def uncut(a):
+        return a.transpose(1, 0, 2).reshape(share, -1)
+
+    def lane(a, at, n):
+        return lax.dynamic_slice_in_dim(a, at * n, n, a.ndim - 1)
+
+    inner_rows = 2 * blocks * half // width
+    owner = mp * dp_size + dp
+    grads = (
+        total[0:3], total[3], uncut(total[4 : 4 + blocks]), uncut(total[4 + blocks :]),
+        lane(sums[0:6], dp, affine.shape[1]),
+        lane(sums[6:8], owner, head_bias.shape[1]),
+        lane(sums[8 : 8 + inner_rows].reshape(-1), owner, inner_bias.shape[0]),
+    )
+    mean_loss = sums[8 + inner_rows, 0] / float(pairing.size * dp_size)
+    weights = (qkv_weight, out_weight, up_weight, down_weight, affine, head_bias, inner_bias)
+    firsts = (qkv_first, out_first, up_first, down_first, affine_first, head_first, inner_first)
+    seconds = (qkv_second, out_second, up_second, down_second, affine_second, head_second, inner_second)
+    decays = (weight_decay, weight_decay, weight_decay, weight_decay, 0.0, 0.0, 0.0)
+    steps = [moments(weights[i], firsts[i], seconds[i], grads[i], decays[i]) for i in range(7)]
+    updates = [s[2] for s in steps]
+    squares = jnp.stack([tensor_squares(*weights, 2.0), tensor_squares(*updates, 2.0)])
+    squares = sum_all(depth, jnp.pad(squares, ((0, 6), (0, 113))))
+    norms = jnp.sqrt(squares[0:2, 0:15])
+    weight_split, update_split = split_norms(norms[0]), split_norms(norms[1])
+    results = [mean_loss, grad_input]
+    for i in range(7):
+        results += [scaled_step(weights[i], updates[i], weight_split[i], update_split[i]), steps[i][0], steps[i][1]]
+    return (*results, norms)
 
 
 def body(
@@ -335,8 +1122,10 @@
 
 
 def solution(mesh):
+    depth = mesh.shape["dp"] // 4
+    fits = mesh.shape["mp"] == 2 and mesh.shape["dp"] % 8 == 0 and 768 // mesh.shape["dp"] % 16 == 0
     return jax.shard_map(
-        body,
+        functools.partial(body_near, depth) if fits else body,
         mesh=mesh,
         in_specs=(
             P("dp", None, None),

time: 1050 us -> 278 us (0.26)
  waiting for transfers between devices: 589 us -> 0 us
  Pallas kernels: 0 us -> 231 us
  blocking collectives: 195 us -> 0 us
  matrix products: 90.4 us -> 0 us
  local copies, waits for them, and re-layouts: 74 us -> 14.8 us
  other arithmetic: 74.1 us -> 23.8 us
  between operations: 24.8 us -> 7.91 us
    pallas_call x0 -> x2, Pallas kernels: none -> 231 us  [the longest x1 218 us: block_step(): pl.pallas_call(functools.partial(block_kernel, depth), out_shape=(jax.Sha...]
    reduce_scatter x3 -> x0, waiting for transfers between devices: 210 us -> none  [the longest x1 75.7 us: body(): lax.psum_scatter(down_grad, 'dp', scatter_dimension=0, tiled=True)]
    psum x4 -> x0, waiting for transfers between devices: 195 us -> none  [the longest x1 51.5 us: body(): lax.psum(jnp.einsum('kte,kde->td', grad_qkv, qkv_full, preferred_element_...]
    all_gather x4 -> x0, waiting for transfers between devices: 112 us -> none  [the longest x1 42 us: body(): lax.all_gather(up_weight.astype(jnp.bfloat16), 'dp', axis=0, tiled=True)]
    psum x2 -> x0, blocking collectives: 103 us -> none  [the longest x1 63.2 us: body(): loss_total = lax.psum(loss_local, 'dp')]
    dot_general x22 -> x0, matrix products: 90.4 us -> none  [the longest x7 32.3 us: summation_axes_spec(): lax.dot_general(left, right, (((left_dim,), (right_dim,)), ((), ())), pre...]
    unnamed x15 -> x0, waiting for transfers between devices: 72.4 us -> none
    all_gather x3 -> x0, blocking collectives: 62.4 us -> none  [the longest x1 23.2 us: body(): lax.all_gather(affine.astype(jnp.bfloat16), 'dp', axis=1, tiled=True)]
  transfers between devices with their start and end apart: 13 -> 0, of which waited for: 11 -> 0; matrix products, arithmetic and copies ran while one was open for 8% -> 0% of each run, Pallas kernels for 0% -> 0%
where the time goes in v1:
time: 278 us; the launch traced here: 277 us
  Pallas kernels  231 us (83%)
  other arithmetic  23.8 us (9%)
  local copies, waits for them, and re-layouts  14.8 us (5%)
  between operations  7.91 us (3%)
    pallas_call x1, Pallas kernels, block_step(): pl.pallas_call(functools.partial(block_kernel, depth), out_shape=(jax.Sha...  218 us
    pallas_call x1, Pallas kernels, sum_all(): pl.pallas_call(functools.partial(sum_kernel, depth), out_shape=jax.ShapeD...  13.2 us
    sub x7, other arithmetic, scaled_step(): return weight - learning_rate * weight_norm / update_norm * update  10.7 us
    concatenate x2, local copies, waits for them, and re-layouts, tensor_squares(): jnp.concatenate([jnp.sum(qkv * qkv, (1, 2)), jnp.sum(out * out)[None], jn...  6.52 us

profile of v1, /device:TPU:0, one launch (start us, length us, event | category | flops | bytes accessed | tf_op | source)
XLA Modules:
  0.0 277.2 jit_solution(7449909762320110087)
XLA Ops:
  0.7 1.3 reshape.165.segment
  1.9 217.5 %train_block.1 = (f32[12,48,384]{2,1,0:T(8,128)}, f32[16,768]{1,0:T(8,128)}, f32[4,256,768]{2,1,0:T(8,128)}) custom-call(bf16[4,256,768]{2,1,0:T(8,128)(2,1)} %tokens.1, s32[4,1,256]{2,1,0:T(1,128)} %reshape.165.segment, s32[4,1,64]{2,1,0:T(1,128)} %bitcast.41, bf16[64,768]{1,0:T(8,128)(2,1)} %images.1, f32[3,48,384]{2,1,0:T(8,128)} %qkv_weight.1, ...), custom_call_target="tpu_custom_call" | custom-call | tf_op jit(solution)/shard_map/train_block/pallas_call | solution.py:763
  219.5 0.0 copy-start.1
  219.5 0.0 copy-start.2
  219.5 0.0 copy-start.4
  219.5 0.0 copy-start.5
  219.5 0.0 copy-start.6
  219.5 0.0 copy-start.7
  219.6 1.3 slice.99
  221.5 2.7 multiply_reduce_fusion.5
  224.2 0.0 copy-start.8
  224.2 0.0 copy-start.9
  224.2 0.0 copy-start.14
  224.2 0.0 copy-start.15
  224.2 0.0 copy-start.13
  224.2 2.4 multiply_reduce_fusion.7
  226.6 1.1 slice_bitcast_fusion
  227.7 0.0 copy-start.3
  227.8 0.0 copy-done.1
  227.8 0.0 copy-done.2
  227.8 0.0 copy-done.4
  227.8 0.0 copy-done.5
  227.8 0.0 copy-done.6
  227.8 0.0 copy-done.7
  227.8 0.0 copy-start
  227.8 2.0 multiply_reduce_fusion.2
  229.9 0.0 copy-done.8
  229.9 0.0 copy-done.9
  229.9 0.0 copy-done.14
  229.9 0.0 copy-done.15
  229.9 0.8 multiply_reduce_fusion.9
  230.7 0.0 copy-start.11
  230.7 0.0 copy-start.12
  230.7 0.5 broadcast_multiply_fusion
  231.2 0.7 slice.105
  232.0 0.0 copy-done.13
  232.0 2.0 multiply_reduce_fusion.10
  234.0 0.7 slice.106
  234.8 1.9 multiply_reduce_fusion.12
  236.7 3.3 %concatenate.7 = f32[15]{0:T(128)S(1)} concatenate(f32[3]{0:T(128)} %get-tuple-element.35, f32[1]{0:T(128)} %bitcast.9, f32[1]{0:T(128)} %bitcast.11, f32[1]{0:T(128)} %bitcast.13, f32[6]{0:T(128)} %get-tuple-element.70, f32[2]{0:T(128)} %get-tuple-element.44, f32[1]{0:T(128)} %bitcast.14), dimensions={0} | concatenate | bytes 120 | tf_op jit(solution)/shard_map/concatenate | solution.py:52
  239.9 3.2 %concatenate.6 = f32[15]{0:T(128)S(1)} concatenate(f32[3]{0:T(128)} %get-tuple-element.34, f32[1]{0:T(128)} %bitcast.3, f32[1]{0:T(128)} %bitcast.4, f32[1]{0:T(128)} %bitcast.5, f32[6]{0:T(128)} %get-tuple-element.71, f32[2]{0:T(128)} %get-tuple-element.68, f32[1]{0:T(128)} %bitcast.6), dimensions={0} | concatenate | bytes 120 | tf_op jit(solution)/shard_map/concatenate | solution.py:52
  243.2 0.6 select_maximum_fusion.own_ref
  243.8 13.2 %sum_squares.1 = f32[8,128]{1,0:T(8,128)} custom-call(f32[8,128]{1,0:T(8,128)} %select_maximum_fusion.own_ref), custom_call_target="tpu_custom_call" | custom-call | tf_op jit(solution)/shard_map/sum_squares/pallas_call | solution.py:801
  257.0 0.7 slice_sqrt_fusion
  257.7 0.0 copy-start.10
  257.7 2.0 multiply_subtract_fusion.2
  259.7 0.6 fusion.19
  261.6 0.0 copy-done.3
  261.6 1.6 multiply_subtract_fusion.3
  264.6 1.9 multiply_subtract_fusion.1
  267.8 2.0 multiply_subtract_fusion
  269.9 0.1 fusion.9
  269.9 0.0 copy-done.11
  269.9 0.0 copy-done.12
  269.9 0.7 multiply_subtract_fusion.4
  270.6 0.1 fusion.10
  270.7 1.3 multiply_subtract_fusion.5
  273.2 1.2 multiply_subtract_fusion.6
  274.4 0.0 copy-done
  274.4 1.7 copy.54
  276.1 0.0 copy-done.10
  (5 shorter events, 0.1 us)
Async XLA Ops:
  219.5 8.3 %copy-start.1 = (f32[48,1536]{1,0:T(8,128)S(1)}, f32[48,1536]{1,0:T(8,128)}, u32[]{:S(2)}) copy-start(f32[48,1536]{1,0:T(8,128)} %up_weight.1) | copy-start | bytes 884740
  219.5 8.3 %copy-start.2 = (f32[48,1536]{1,0:T(8,128)S(1)}, f32[48,1536]{1,0:T(8,128)}, u32[]{:S(2)}) copy-start(f32[48,1536]{1,0:T(8,128)} %down_weight.1) | copy-start | bytes 884740
  219.5 8.3 %copy-start.4 = (f32[48,1536]{1,0:T(8,128)S(1)}, f32[48,1536]{1,0:T(8,128)}, u32[]{:S(2)}) copy-start(f32[48,1536]{1,0:T(8,128)} %param.39) | copy-start | bytes 884740
  219.5 8.3 %copy-start.5 = (f32[48,1536]{1,0:T(8,128)S(1)}, f32[48,1536]{1,0:T(8,128)}, u32[]{:S(2)}) copy-start(f32[48,1536]{1,0:T(8,128)} %param.40) | copy-start | bytes 884740
  219.5 8.3 %copy-start.6 = (f32[48,1536]{1,0:T(8,128)S(1)}, f32[48,1536]{1,0:T(8,128)}, u32[]{:S(2)}) copy-start(f32[48,1536]{1,0:T(8,128)} %param.37) | copy-start | bytes 884740
  219.5 8.3 %copy-start.7 = (f32[48,1536]{1,0:T(8,128)S(1)}, f32[48,1536]{1,0:T(8,128)}, u32[]{:S(2)}) copy-start(f32[48,1536]{1,0:T(8,128)} %param.36) | copy-start | bytes 884740
  224.2 5.6 %copy-start.8 = (f32[16,768]{1,0:T(8,128)S(1)}, f32[16,768]{1,0:T(8,128)}, u32[]{:S(2)}) copy-start(f32[16,768]{1,0:T(8,128)} %get-tuple-element.27) | copy-start | bytes 147460
  224.2 5.6 %copy-start.9 = (f32[6,48]{1,0:T(8,128)S(1)}, f32[6,48]{1,0:T(8,128)}, u32[]{:S(2)}) copy-start(f32[6,48]{1,0:T(8,128)} %affine.1) | copy-start | bytes 3460
  224.2 5.6 %copy-start.14 = (f32[6,48]{1,0:T(8,128)S(1)}, f32[6,48]{1,0:T(8,128)}, u32[]{:S(2)}) copy-start(f32[6,48]{1,0:T(8,128)} %param.42) | copy-start | bytes 3460
  224.2 5.6 %copy-start.15 = (f32[6,48]{1,0:T(8,128)S(1)}, f32[6,48]{1,0:T(8,128)}, u32[]{:S(2)}) copy-start(f32[6,48]{1,0:T(8,128)} %param.43) | copy-start | bytes 3460
  224.2 7.7 %copy-start.13 = (f32[2,24]{1,0:T(2,128)S(1)}, f32[2,24]{1,0:T(2,128)}, u32[]{:S(2)}) copy-start(f32[2,24]{1,0:T(2,128)} %head_bias.1) | copy-start | bytes 580
  227.7 33.9 %copy-start.3 = (f32[48,384]{1,0:T(8,128)S(1)}, f32[48,384]{1,0:T(8,128)}, u32[]{:S(2)}) copy-start(f32[48,384]{1,0:T(8,128)} %out_weight.1) | copy-start | bytes 221188
  227.8 46.6 %copy-start = (f32[4,256,768]{2,1,0:T(8,128)S(1)}, f32[4,256,768]{2,1,0:T(8,128)}, u32[]{:S(2)}) copy-start(f32[4,256,768]{2,1,0:T(8,128)} %get-tuple-element.101) | copy-start | bytes 9437188
  230.7 39.2 %copy-start.11 = (f32[6,48]{1,0:T(8,128)S(1)}, f32[6,48]{1,0:T(8,128)}, u32[]{:S(2)}) copy-start(f32[6,48]{1,0:T(8,128)} %get-tuple-element.115) | copy-start | bytes 3460
  230.7 39.2 %copy-start.12 = (f32[6,48]{1,0:T(8,128)S(1)}, f32[6,48]{1,0:T(8,128)}, u32[]{:S(2)}) copy-start(f32[6,48]{1,0:T(8,128)} %get-tuple-element.116) | copy-start | bytes 3460
  257.7 18.4 %copy-start.10 = (f32[2,15]{1,0:T(2,128)}, f32[2,15]{1,0:T(2,128)S(1)}, u32[]{:S(2)}) copy-start(f32[2,15]{1,0:T(2,128)S(1)} %slice_sqrt_fusion) | copy-start | bytes 364

commit v2 on v1

--- a/solution.py
+++ b/solution.py
@@ -81,6 +81,7 @@
 MESH = pl.DeviceIdType.MESH
 f32 = jnp.float32
 bf16 = jnp.bfloat16
+AHEAD, GLAG, RLAG, NROWS = 3, 1, 1, 32
 
 
 class Place:
@@ -106,12 +107,16 @@
     def over_z(self, k):
         return self.at(lax.rem(self.z + k, self.depth), self.y, self.c, self.x)
 
-    def barrier(self):
+    def in_plane(self, d):
+        return self.at(self.z, 1 - self.y if d & 4 else self.y, 1 - self.c if d & 2 else self.c, 1 - self.x if d & 1 else self.x)
+
+    def greet(self):
         sem = pltpu.get_barrier_semaphore()
-        peers = [self.over_x(), self.over_y(), self.over_c()] + [self.over_z(k) for k in range(1, self.depth)]
-        for peer in peers:
+        for peer in [self.in_plane(d) for d in range(1, 8)] + [self.over_z(k) for k in range(1, self.depth)]:
             pl.semaphore_signal(sem, inc=1, device_id=peer, device_id_type=MESH)
-        pl.semaphore_wait(sem, len(peers))
+
+    def meet(self):
+        pl.semaphore_wait(pltpu.get_barrier_semaphore(), 7 + self.depth - 1)
 
 
 class Wire:
@@ -139,6 +144,27 @@
         copy.wait_recv()
 
 
+class Flow:
+    def __init__(self, stages, lags):
+        self.stages, self.lags, self.done = stages, lags, [0] * len(stages)
+
+    def run(self, s):
+        self.stages[s](self.done[s])
+        self.done[s] += 1
+
+    def pump(self, lags=None):
+        moved = False
+        for s in range(len(self.stages) - 1, 0, -1):
+            if self.done[s] < self.done[s - 1] - (self.lags if lags is None else lags)[s]:
+                self.run(s)
+                moved = True
+        return moved
+
+    def drain(self):
+        while self.pump([0] * len(self.stages)):
+            pass
+
+
 class Sheet:
     def __init__(self, full, u):
         self.full, self.u, self.half = full, u, full.shape[-1] // 2
@@ -148,22 +174,11 @@
         return self.full.at[self.u, z, y, c, :, lanes]
 
 
-class Stack:
-    def __init__(self, full):
-        self.full = full
-
-    def part(self, z, y, c, x=None):
-        return self.full.at[z, y, c, slice(None) if x is None else x]
-
-
 class Gather:
     def __init__(self, place, wire, items, ahead, lag):
-        self.p, self.wire, self.items, self.ahead, self.lag = place, wire, items, ahead, lag
+        self.p, self.wire, self.items, self.ahead = place, wire, items, ahead
         self.flight = {}
-        self.t = 0
-        self.whole = -1
-        for i in range(min(ahead, len(items))):
-            self.far(i)
+        self.flow = Flow([self.far, self.one, self.two, self.core, self.whole], [0, 0, lag, lag, 1])
 
     def far(self, i):
         p, it = self.p, self.items[i]
@@ -190,23 +205,25 @@
         r = it.part(slice(None), slice(None), p.c)
         self.flight["c", i] = [self.wire.start(r, r, p.over_c())]
 
+    def whole(self, i):
+        arrive(self.flight["c", i])
+
+    def begin(self):
+        flow, n = self.flow, len(self.items)
+        while flow.done[0] < min(flow.done[1] + self.ahead, n):
+            flow.run(0)
+
     def step(self):
-        t, n, lag = self.t, len(self.items), self.lag
-        if t < n:
-            self.one(t)
-            if t + self.ahead < n:
-                self.far(t + self.ahead)
-        if 0 <= t - lag < n:
-            self.two(t - lag)
-        if 0 <= t - 2 * lag < n:
-            self.core(t - 2 * lag)
-        if 0 <= t - 2 * lag - 1 < n:
-            arrive(self.flight["c", t - 2 * lag - 1])
-            self.whole = t - 2 * lag - 1
-        self.t += 1
+        flow, n = self.flow, len(self.items)
+        while flow.done[0] < min(flow.done[1] + self.ahead, n):
+            flow.run(0)
+        moved = flow.pump([0] * 5 if flow.done[1] == n else None)
+        while flow.done[0] < min(flow.done[1] + self.ahead, n):
+            flow.run(0)
+        return moved
 
     def until(self, i):
-        while self.whole < i:
+        while self.flow.done[4] <= i:
             self.step()
 
 
@@ -220,15 +237,15 @@
 
 
 class Reduce:
-    def __init__(self, place, wire, order, lag, free, part, from_core, one_a, one_b, two_a, two_b, from_z, total):
-        self.p, self.wire, self.order, self.lag, self.free = place, wire, order, lag, free
+    def __init__(self, place, wire, order, lag, free, part, from_core, one_a, one_b, two_a, two_b, from_z, total, use):
+        self.p, self.wire, self.order, self.free, self.use = place, wire, order, free, use
         self.part, self.from_core, self.one_a, self.one_b = part, from_core, one_a, one_b
         self.two_a, self.two_b, self.from_z, self.total = two_a, two_b, from_z, total
         self.h = place.depth // 2
         self.half = part.shape[-1] // 2
         self.slots = from_core.shape[0]
         self.flight = {}
-        self.t = 0
+        self.flow = Flow([self.core, self.one, self.two, self.far, self.last], [0, 1, lag, lag, lag])
 
     def lanes(self, x):
         return pl.ds(pl.multiple_of(x * self.half, 128), self.half)
@@ -282,18 +299,17 @@
         for j in range(p.depth - 1):
             t = t + self.from_z[j, u].astype(f32)
         self.total[u] = t
+        self.use(u, t)
 
     def step(self):
-        t, n, lag = self.t, len(self.order), self.lag
-        stages = ((self.core, 0), (self.one, 1), (self.two, 1 + lag), (self.far, 1 + 2 * lag), (self.last, 1 + 3 * lag))
-        for stage, late in stages:
-            if 0 <= t - late < n:
-                stage(t - late)
-        self.t += 1
+        self.flow.run(0)
+        self.flow.pump()
+
+    def pump(self):
+        self.flow.pump()
 
     def finish(self):
-        while self.t < len(self.order) + 1 + 3 * self.lag:
-            self.step()
+        self.flow.drain()
 
 
 class SumAll:
@@ -331,13 +347,58 @@
             self.finish()
 
 
+class SumSoon:
+    def __init__(self, place, wire, own, plane, line):
+        p = place
+        slot = (p.y * 2 + p.c) * 2 + p.x
+        plane[slot] = own[...]
+        arrive([wire.start(own, plane.at[slot], p.in_plane(d)) for d in range(1, 8)])
+        value = plane[0]
+        for d in range(1, 8):
+            value = value + plane[d]
+        line[p.z] = value
+        arrive([wire.start(line.at[p.z], line.at[p.z], p.over_z(k)) for k in range(1, p.depth)])
+        value = line[0]
+        for z in range(1, p.depth):
+            value = value + line[z]
+        self.value = value
+
+
+class Pictures:
+    def __init__(self, place, wire, full):
+        self.p, self.wire, self.full = place, wire, full
+        mine = full.at[place.z, place.y, place.c]
+        self.flight = [wire.start(mine, mine, place.over_y())]
+        self.sent = 0
+
+    def far(self):
+        p = self.p
+        if self.sent == 0:
+            arrive(self.flight)
+            self.flight = []
+        mine = self.full.at[p.z, :, p.c]
+        self.sent += 1
+        self.flight.append(self.wire.start(mine, mine, p.over_z(self.sent)))
+
+    def core(self):
+        p = self.p
+        while self.sent < p.depth - 1:
+            self.far()
+        arrive(self.flight)
+        r = self.full.at[:, :, p.c]
+        self.flight = [self.wire.start(r, r, p.over_c())]
+
+    def whole(self):
+        arrive(self.flight)
+
+
 def dot(a, b, left=1, right=0):
     return lax.dot_general(a, b, (((left,), (right,)), ((), ())), preferred_element_type=f32)
 
 
-def row_loop(count, size, f):
+def row_loop(count, size, f, start=0):
     def step(i, carry):
-        f(pl.ds(pl.multiple_of(i * size, size), size))
+        f(pl.ds(pl.multiple_of(start + i * size, size), size))
         return carry
 
     lax.fori_loop(0, count // size, step, 0)
@@ -359,33 +420,58 @@
     return jnp.sum(x.reshape(x.shape[0] // 8, 8, x.shape[1]), 0)
 
 
+def placing(n, at, lanes):
+    spot = lax.broadcasted_iota(jnp.int32, (n, lanes), 1) == lax.broadcasted_iota(jnp.int32, (n, lanes), 0) + at
+    return jnp.where(spot, 1.0, 0.0).astype(bf16)
+
+
+def picked(a, at, n):
+    spot = placing(n, at, a.shape[1])
+    return sum(dot(term, spot, 1, 1) for term in three(a))
+
+
+def row_of(a, at):
+    rows = lax.broadcasted_iota(jnp.int32, a.shape, 0) == at
+    return jnp.sum(jnp.where(rows, a, jnp.zeros_like(a)), 0, keepdims=True)
+
+
 def block_kernel(
     depth,
     tokens, segment, pairing, images, qkv_weight, out_weight, up_weight, down_weight, affine, head_bias, inner_bias,
-    total, sums, grad_input,
+    qkv_first, qkv_second, out_first, out_second, up_first, up_second, down_first, down_second,
+    affine_first, affine_second, head_first, head_second, inner_first, inner_second,
+    total, small_grad, norms, grad_low,
     full, pictures, part, from_core, one_a, one_b, two_a, two_b, from_z,
     tok, normed_one, qkv, mixed, resid, normed_two, hidden, slope, stream, grad_mixed, acc, low,
-    probs, same, wide, room, room2, folds, cap, key_acc, value_acc, grad_near, grad_far,
-    send, recv, free, local,
+    probs, same, wide, sums, room, room2, folds, cap,
+    old_qkv, old_out, old_up, old_down, squares, tile_sums, plane, line,
+    send, recv, free, local, local_old,
 ):
     place = Place(depth)
+    place.greet()
     x, dp = place.x, place.dp
     rows, width = tok.shape
     packs, length = 2, rows // 2
     half = qkv_weight.shape[2]
     units = full.shape[0]
+    share = full.shape[4]
     blocks = up_weight.shape[1] // half
-    share = full.shape[4]
     up0, down0 = 4, 4 + blocks
 
     token_copies = [
         pltpu.make_async_copy(tokens.at[packs * x + p], tok.at[pl.ds(p * length, length)], local.at[p]) for p in range(packs)
     ]
-    for copy in token_copies:
+    pairs_old = ((qkv_first, qkv_second, old_qkv), (out_first, out_second, old_out), (up_first, up_second, old_up), (down_first, down_second, old_down))
+    old_copies = []
+    for i, (one, two, kept) in enumerate(pairs_old):
+        old_copies += [pltpu.make_async_copy(one, kept.at[0], local_old.at[2 * i]), pltpu.make_async_copy(two, kept.at[1], local_old.at[2 * i + 1])]
+    for copy in token_copies + old_copies:
         copy.start()
 
+    mine_lanes = pl.ds(pl.multiple_of(x * half, 128), half)
+
     def keep(u, value):
-        full[u, place.z, place.y, place.c, :, pl.ds(pl.multiple_of(x * half, 128), half)] = value.astype(bf16)
+        full[u, place.z, place.y, place.c, :, mine_lanes] = value.astype(bf16)
 
     for k in range(3):
         keep(k, qkv_weight[k])
@@ -393,72 +479,65 @@
     for j in range(blocks):
         keep(up0 + j, up_weight[:, j * half : (j + 1) * half])
         keep(down0 + j, down_weight[:, j * half : (j + 1) * half])
-    few = pictures.shape[4]
-    picture = images[pl.ds(pl.multiple_of(x * few, few), few)].astype(f32)
-    pictures[place.z, place.y, place.c, x] = normalize(picture).astype(bf16)
-
-    place.barrier()
+    pictures[place.z, place.y, place.c] = normalize(images[...].astype(f32)).astype(bf16)
+
+    place.meet()
     wire = Wire(send, recv)
-    items = [Sheet(full, u) for u in range(units)]
-    items.insert(units - 1, Stack(pictures))
-    image_at = units - 1
-    gather = Gather(place, wire, items, 3, 2)
-
-    def ready(u):
-        gather.until(u if u < image_at else u + 1)
-
-    def placed(a, at, lanes):
-        a = a.astype(bf16)
-        n = a.shape[1]
-        spot = lax.broadcasted_iota(jnp.int32, (n, lanes), 1) == lax.broadcasted_iota(jnp.int32, (n, lanes), 0) + at
-        return dot(a, jnp.where(spot, 1.0, 0.0).astype(bf16))
+    gather = Gather(place, wire, [Sheet(full, u) for u in range(units)], AHEAD, GLAG)
+    ready = gather.until
+    gather.begin()
+    scenes = Pictures(place, wire, pictures)
 
     owner = x * (4 * depth) + dp
     n_affine, n_head, n_inner = affine.shape[1], head_bias.shape[1], inner_bias.shape[1]
+    first = jnp.where(x == 0, 1.0, 0.0)
+    inner_rows = 2 * blocks * half // width
+    inner_at, inner_row = (owner * n_inner) % width, (owner * n_inner) // width
     wide[...] = jnp.zeros_like(wide)
-    first = jnp.where(x == 0, 1.0, 0.0)
-    wide[0:6] = placed(affine[...], dp * n_affine, width) * first
-    wide[6:8] = placed(head_bias[...], owner * n_head, width)
-    inner_row = placed(inner_bias[...], (owner * n_inner) % width, width)
-    inner_rows = 2 * blocks * half // width
-    at_row = lax.broadcasted_iota(jnp.int32, (inner_rows, width), 0) == (owner * n_inner) // width
-    wide[8 : 8 + inner_rows] = jnp.where(at_row, jnp.broadcast_to(inner_row, (inner_rows, width)), 0.0)
+    wide[0:6] = dot(affine[...].astype(bf16), placing(n_affine, dp * n_affine, width)) * first
+    wide[6:8] = dot(head_bias[...].astype(bf16), placing(n_head, owner * n_head, width))
+    inner_wide = dot(inner_bias[...].astype(bf16), placing(n_inner, inner_at, width))
+    at_row = lax.broadcasted_iota(jnp.int32, (inner_rows, width), 0) == inner_row
+    wide[8 : 8 + inner_rows] = jnp.where(at_row, jnp.broadcast_to(inner_wide, (inner_rows, width)), 0.0)
     spread = SumAll(place, wire, wide, room)
-    while spread.stage < 4:
-        spread.start()
-        if gather.t < 1:
-            gather.step()
-        spread.finish()
-
-    for copy in token_copies:
-        copy.wait()
-
-    slots = pairing.shape[2]
+    spread.start()
+
+    slots = pairing.shape[1]
     tile, window = 64, 128
     starts = [min(max(t * tile - (window - tile) // 2, 0), length - window) for t in range(length // tile)]
-    onehots, columns = [], []
+    onehots = []
     for p in range(packs):
-        seg = jnp.broadcast_to(segment[packs * x + p], (slots, length))
+        seg = jnp.broadcast_to(row_of(segment[...], packs * x + p), (slots, length))
         onehot = jnp.where(seg == lax.broadcasted_iota(jnp.int32, (slots, length), 0), 1.0, 0.0)
         onehots.append(onehot)
         low_hot = onehot.astype(bf16)
-        both = dot(low_hot, low_hot, 0, 0)
-        folds_at = acc.at[pl.ds(0, length), pl.ds(0, length)]
-        folds_at[...] = both
-        eye = lax.broadcasted_iota(jnp.int32, (window, window), 0) == lax.broadcasted_iota(jnp.int32, (window, window), 1)
+        both = acc.at[pl.ds(0, length), pl.ds(0, length)]
+        both[...] = dot(low_hot, low_hot, 0, 0)
         for t, w in enumerate(starts):
-            pick = lax.broadcasted_iota(jnp.int32, (length, window), 0) == lax.broadcasted_iota(jnp.int32, (length, window), 1) + w
-            shared = dot(folds_at[pl.ds(t * tile, tile)].astype(bf16), jnp.where(pick, 1.0, 0.0).astype(bf16))
+            shared = dot(both[pl.ds(t * tile, tile)].astype(bf16), placing(window, w, length), 1, 1)
             same[p, t, 0:tile] = shared
             same[p, t, tile : 2 * tile] = shared
-
+        if p == 0:
+            spread.finish()
+            spread.start()
     gather.step()
+    spread.finish()
+    spread.start()
+    gather.step()
+    spread.finish()
+    spread.start()
+    gather.step()
+    scenes.far()
+    spread.finish()
+
+    for copy in token_copies:
+        copy.wait()
 
     def norm_one(r):
         center, scale = center_scale(tok[r].astype(f32))
         normed_one[r] = (center * scale * wide[0:1] + wide[1:2]).astype(bf16)
 
-    row_loop(rows, 32, norm_one)
+    row_loop(rows, NROWS, norm_one)
     gather.step()
 
     def unit(u):
@@ -478,6 +557,7 @@
                 row = 6 if k == 0 else 7
                 value = value + wide[row : row + 1, lanes]
             qkv[k, :, lanes] = value.astype(bf16)
+    scenes.far()
 
     root_scale = HD**-0.5
     pair = 2 * HD
@@ -491,29 +571,38 @@
     def joined(a):
         return jnp.where(lower, a[:tile], a[tile:])
 
-    def attend(p):
+    def attend(p, g):
+        lanes = pl.ds(pl.multiple_of(g * pair, pair), pair)
+        span = pl.ds(p * length, length)
+        query, keys, values = qkv[0, span, lanes], qkv[1, span, lanes], qkv[2, span, lanes]
+        found, weights = [], []
+        for t, w in enumerate(starts):
+            scores = dot(doubled(query[t * tile : (t + 1) * tile]), keys[w : w + window], 1, 1) * root_scale
+            scores = jnp.where(same[p, t] > 0.5, scores, mask_value)
+            e = jnp.exp(scores - jnp.max(scores, -1, keepdims=True))
+            prob = (e * (1.0 / jnp.sum(e, -1, keepdims=True))).astype(bf16)
+            weights.append(prob)
+            found.append(joined(dot(prob, values[w : w + window])).astype(bf16))
+        for t in range(len(starts)):
+            probs[p, g, t] = weights[t]
+        mixed[span, lanes] = jnp.concatenate(found, 0)
+
+    def each_pair(f, p, some):
         def step(g, carry):
-            lanes = pl.ds(pl.multiple_of(g * pair, pair), pair)
-            for t, w in enumerate(starts):
-                near = pl.ds(p * length + t * tile, tile)
-                reach = pl.ds(p * length + w, window)
-                query = doubled(qkv[0, near, lanes])
-                scores = dot(query, qkv[1, reach, lanes], 1, 1) * root_scale
-                scores = jnp.where(same[p, t] > 0.5, scores, mask_value)
-                e = jnp.exp(scores - jnp.max(scores, -1, keepdims=True))
-                prob = (e * (1.0 / jnp.sum(e, -1, keepdims=True))).astype(bf16)
-                probs[p, g, t] = prob
-                mixed[near, lanes] = joined(dot(prob, qkv[2, reach, lanes])).astype(bf16)
+            f(p, g)
             return carry
 
-        lax.fori_loop(0, pairs, step, 0)
+        lax.fori_loop(some[0], some[1], step, 0)
 
     for p in range(packs):
-        attend(p)
-        gather.step()
+        for some in ((0, pairs // 2), (pairs // 2, pairs)):
+            each_pair(attend, p, some)
+            gather.step()
+    scenes.far()
 
     ready(3)
     acc[...] = dot(mixed[...], unit(3), 1, 1)
+    gather.step()
 
     def norm_two(r):
         value = tok[r].astype(f32) + acc[r] + wide[4:5]
@@ -522,17 +611,16 @@
         normed_two[r] = (center * scale * wide[2:3] + wide[3:4]).astype(bf16)
         stream[r] = value + wide[5:6]
 
-    row_loop(rows, 32, norm_two)
+    row_loop(rows, NROWS, norm_two)
+
+    def inner_lanes(j):
+        at = j * half
+        return ((8 + at // width, at % width), (8 + (blocks * half + at) // width, (blocks * half + at) % width))
 
     curve = (2.0 / jnp.pi) ** 0.5
     for j in range(blocks):
         ready(up0 + j)
-        at = j * half
-        row, lane = at // width, at % width
-        rows_per = blocks * half // width
-        bias = jnp.concatenate(
-            [wide[8 + row : 9 + row, lane : lane + half], wide[8 + rows_per + row : 9 + rows_per + row, lane : lane + half]], 1
-        )
+        bias = jnp.concatenate([wide[row : row + 1, lane : lane + half] for row, lane in inner_lanes(j)], 1)
         for k in range(width // chunk):
             lanes = pl.ds(k * chunk, chunk)
             acc[:, lanes] = dot(normed_two[...], unit_lanes(up0 + j, k))
@@ -545,12 +633,15 @@
             slope[j, r] = (0.5 * (1.0 + t) + 0.5 * u * (1.0 - t * t) * (curve * (1.0 + 3.0 * 0.044715 * square))).astype(bf16)
 
         row_loop(rows, 16, activate)
+        if j == 1:
+            scenes.core()
 
     for j in range(blocks):
         ready(down0 + j)
         stream[...] += dot(hidden[j], unit(down0 + j), 1, 1)
-
-    live_rows, count_rows, target_rows = [], [], []
+    scenes.whole()
+
+    count_rows, target_rows = [], []
     for p in range(packs):
         count = jnp.sum(onehots[p], 1, keepdims=True)
         hot = onehots[p].astype(bf16)
@@ -558,7 +649,7 @@
         pooled = dot(hot, hi) + dot(hot, mid) + dot(hot, lo)
         cap[pl.ds(p * slots, slots)] = pooled / jnp.maximum(count, 1.0)
         count_rows.append(count)
-        names = jnp.broadcast_to(pairing[packs * x + p], (slots, slots)).astype(f32)
+        names = jnp.broadcast_to(row_of(pairing[...], packs * x + p), (slots, slots)).astype(f32)
         diagonal = lax.broadcasted_iota(jnp.int32, (slots, slots), 0) == lax.broadcasted_iota(jnp.int32, (slots, slots), 1)
         target_rows.append(jnp.sum(jnp.where(diagonal, names, 0.0), 1, keepdims=True))
     counts = jnp.concatenate(count_rows, 0)
@@ -568,7 +659,6 @@
     radius = lax.rsqrt(jnp.sum(pooled * pooled, -1, keepdims=True) + norm_epsilon)
     caption = (pooled * radius).astype(bf16)
     all_images = pictures[...].reshape(-1, width)
-    count = all_images.shape[0]
     logits = sharpness_divisor * dot(caption, all_images, 1, 1)
     hit = lax.broadcasted_iota(jnp.int32, logits.shape, 1).astype(f32) == target
     best = jnp.max(logits, -1, keepdims=True)
@@ -577,8 +667,7 @@
     positive = jnp.sum(jnp.where(hit, logits, 0.0), -1, keepdims=True)
     cross = best + jnp.log(sum_e) - positive
     loss = jnp.sum(live * cross, 0, keepdims=True)
-    scaled = loss_scale * live
-    grad_logits = (scaled * (e * (1.0 / sum_e) - jnp.where(hit, 1.0, 0.0))).astype(bf16)
+    grad_logits = (loss_scale * live * (e * (1.0 / sum_e) - jnp.where(hit, 1.0, 0.0))).astype(bf16)
     grad_caption = sharpness_divisor * dot(grad_logits, all_images)
     inner = jnp.sum(pooled * grad_caption, -1, keepdims=True)
     grad_pooled = radius * grad_caption - (radius * radius * radius) * inner * pooled
@@ -596,8 +685,30 @@
 
     row_loop(rows, 32, lower_stream)
 
+    squares[...] = jnp.zeros_like(squares)
+    for copy in old_copies:
+        copy.wait()
+
+    def lanes_folded(a):
+        a = fold(a)
+        return sum(a[:, i * 128 : (i + 1) * 128] for i in range(a.shape[1] // 128))
+
+    def use(u, grad):
+        if u < 3:
+            weight, one, two, row = qkv_weight[u], old_qkv[0, u], old_qkv[1, u], u
+        elif u == 3:
+            weight, one, two, row = out_weight[...], old_out[0], old_out[1], 3
+        else:
+            row = 4 if u < down0 else 5
+            at = (u - up0) % blocks * half
+            weights, kept = (up_weight, old_up) if row == 4 else (down_weight, old_down)
+            weight, one, two = weights[:, at : at + half], kept[0, :, at : at + half], kept[1, :, at : at + half]
+        update = moments(weight, one, two, grad, weight_decay)[2]
+        squares[0, row] += lanes_folded(weight * weight)
+        squares[1, row] += lanes_folded(update * update)
+
     order = [down0 + j for j in range(blocks)] + [up0 + j for j in range(blocks)] + [3, 0, 1, 2]
-    reduce = Reduce(place, wire, order, 2, free, part, from_core, one_a, one_b, two_a, two_b, from_z, total)
+    reduce = Reduce(place, wire, order, RLAG, free, part, from_core, one_a, one_b, two_a, two_b, from_z, total, use)
 
     def weight_grad(u, left, right):
         for j in range(width // chunk):
@@ -621,11 +732,8 @@
         folds[6] = jnp.zeros_like(folds[6])
         row_loop(rows, 32, upper_back)
         inner_sum = jnp.sum(folds[6], 0, keepdims=True)
-        at = j * half
-        row, lane = at // width, at % width
-        rows_per = blocks * half // width
-        sums[8 + row : 9 + row, lane : lane + half] = inner_sum[:, :half]
-        sums[8 + rows_per + row : 9 + rows_per + row, lane : lane + half] = inner_sum[:, half:]
+        for i, (row, lane) in enumerate(inner_lanes(j)):
+            sums[row : row + 1, lane : lane + half] = inner_sum[:, i * half : (i + 1) * half]
 
     for j in range(blocks):
         weight_grad(up0 + j, normed_two[...], lambda lanes, j=j: hidden[j, :, lanes])
@@ -649,39 +757,45 @@
         folds[3] += fold(grad)
         folds[4] += fold(value)
 
-    row_loop(rows, 32, norm_two_back)
+    row_loop(rows, NROWS, norm_two_back)
+    reduce.pump()
     weight_grad(3, low[...], lambda lanes: mixed[:, lanes])
     for k in range(width // chunk):
         lanes = pl.ds(k * chunk, chunk)
         grad_mixed[:, lanes] = dot(low[...], unit_lanes(3, k)).astype(bf16)
-
-    def attend_back(p):
-        def step(g, carry):
-            lanes = pl.ds(pl.multiple_of(g * pair, pair), pair)
-            key_acc[...] = jnp.zeros_like(key_acc)
-            value_acc[...] = jnp.zeros_like(value_acc)
-            for t, w in enumerate(starts):
-                near = pl.ds(p * length + t * tile, tile)
-                reach = pl.ds(p * length + w, window)
-                query = doubled(qkv[0, near, lanes])
-                grad = doubled(grad_mixed[near, lanes])
-                prob = probs[p, g, t]
-                prob_wide = prob.astype(f32)
-                grad_prob = dot(grad, qkv[2, reach, lanes], 1, 1)
-                grad_score = prob_wide * (grad_prob - jnp.sum(prob_wide * grad_prob, -1, keepdims=True))
-                grad_score = grad_score.astype(bf16)
-                key_acc[pl.ds(w, window)] += dot(grad_score, query, 0, 0)
-                value_acc[pl.ds(w, window)] += dot(prob, grad, 0, 0)
-                qkv[0, near, lanes] = (joined(dot(grad_score, qkv[1, reach, lanes])) * root_scale).astype(bf16)
-            span = pl.ds(p * length, length)
-            qkv[1, span, lanes] = (key_acc[...] * root_scale).astype(bf16)
-            qkv[2, span, lanes] = value_acc[...].astype(bf16)
-            return carry
-
-        lax.fori_loop(0, pairs, step, 0)
+    reduce.pump()
+
+    def overlaid(pieces):
+        step = 32
+        found = []
+        for at in range(0, length, step):
+            found.append(sum(piece[at - w : at - w + step] for w, piece in zip(starts, pieces) if w <= at < w + window))
+        return jnp.concatenate(found, 0)
+
+    def attend_back(p, g):
+        lanes = pl.ds(pl.multiple_of(g * pair, pair), pair)
+        span = pl.ds(p * length, length)
+        query, keys, values, grads = qkv[0, span, lanes], qkv[1, span, lanes], qkv[2, span, lanes], grad_mixed[span, lanes]
+        of_query, of_keys, of_values = [], [], []
+        for t, w in enumerate(starts):
+            some = doubled(query[t * tile : (t + 1) * tile])
+            grad = doubled(grads[t * tile : (t + 1) * tile])
+            prob = probs[p, g, t]
+            prob_wide = prob.astype(f32)
+            grad_prob = dot(grad, values[w : w + window], 1, 1)
+            grad_score = prob_wide * (grad_prob - jnp.sum(prob_wide * grad_prob, -1, keepdims=True))
+            grad_score = grad_score.astype(bf16)
+            of_keys.append(dot(grad_score, some, 0, 0))
+            of_values.append(dot(prob, grad, 0, 0))
+            of_query.append((joined(dot(grad_score, keys[w : w + window])) * root_scale).astype(bf16))
+        qkv[0, span, lanes] = jnp.concatenate(of_query, 0)
+        qkv[1, span, lanes] = (overlaid(of_keys) * root_scale).astype(bf16)
+        qkv[2, span, lanes] = overlaid(of_values).astype(bf16)
 
     for p in range(packs):
-        attend_back(p)
+        for some in ((0, pairs // 2), (pairs // 2, pairs)):
+            each_pair(attend_back, p, some)
+            reduce.pump()
 
     for k in range(3):
         weight_grad(k, normed_one[...], lambda lanes, k=k: qkv[k, :, lanes])
@@ -690,12 +804,6 @@
             acc[...] = value
         else:
             acc[...] += value
-
-    def head_sums(r):
-        folds[7] += fold(qkv[0, r].astype(f32))
-        folds[8] += fold(qkv[2, r].astype(f32))
-
-    row_loop(rows, 32, head_sums)
 
     def norm_one_back(r):
         center, scale = center_scale(tok[r].astype(f32))
@@ -705,46 +813,67 @@
         value = stream[r] + scale * (
             weighted - jnp.mean(weighted, -1, keepdims=True) - hat * jnp.mean(weighted * hat, -1, keepdims=True)
         )
-        grad_near[r] = value.astype(bf16)
+        low[r] = value.astype(bf16)
         folds[0] += fold(grad * hat)
         folds[1] += fold(grad)
 
-    row_loop(rows, 32, norm_one_back)
-    swap = wire.start(grad_near, grad_far, place.over_x())
-
+    swaps, outs = [], []
+    for p in range(packs):
+        row_loop(length, NROWS, norm_one_back, p * length)
+        mine, there = low.at[pl.ds(p * length, length)], grad_low.at[packs * x + p]
+        swaps.append(wire.start(mine, there, place.over_x()))
+        outs.append(pltpu.make_async_copy(mine, there, local.at[p]))
+        outs[-1].start()
+        reduce.pump()
+
+    def head_sums(r):
+        folds[7] += fold(qkv[0, r].astype(f32))
+        folds[8] += fold(qkv[2, r].astype(f32))
+
+    row_loop(rows, 32, head_sums)
     for k, row in ((0, 0), (1, 1), (2, 2), (3, 3), (4, 4), (5, 5), (7, 6), (8, 7)):
         sums[row : row + 1] = jnp.sum(folds[k], 0, keepdims=True)
     last_row = 8 + inner_rows
     sums[last_row : last_row + 1] = jnp.broadcast_to(loss, (1, width))
-    SumAll(place, wire, sums, room2).run()
-
-    def widen(source, target):
-        def f(r):
-            target[r] = source[r].astype(f32)
-
-        row_loop(rows, 32, f)
-
-    widen(grad_near, acc)
-    outs = [
-        pltpu.make_async_copy(acc.at[pl.ds(p * length, length)], grad_input.at[packs * x + p], local.at[p]) for p in range(packs)
-    ]
-    for copy in outs:
-        copy.start()
+    small_sum = SumAll(place, wire, sums, room2)
+    while small_sum.stage < 4:
+        small_sum.start()
+        reduce.pump()
+        small_sum.finish()
+
+    small_grad[...] = jnp.zeros_like(small_grad)
+    tile_sums[...] = jnp.zeros_like(tile_sums)
+    of_affine = picked(sums[0:6], dp * n_affine, n_affine)
+    of_head = picked(sums[6:8], owner * n_head, n_head)
+    of_inner = picked(row_of(sums[8 : 8 + inner_rows], inner_row), inner_at, n_inner)
+    small_grad[0:6, 0:n_affine] = of_affine
+    small_grad[6:8, 0:n_head] = of_head
+    small_grad[8:9, 0:n_inner] = of_inner
+    small_grad[9:10] = sums[last_row : last_row + 1, 0:128]
+    smalls = (
+        (6, 6, n_affine, affine[...], affine_first[...], affine_second[...], of_affine, first),
+        (12, 2, n_head, head_bias[...], head_first[...], head_second[...], of_head, 1.0),
+        (14, 1, n_inner, inner_bias[...], inner_first[...], inner_second[...], of_inner, 1.0),
+    )
+    for row, n, lanes, weight, one, two, grad, share_of in smalls:
+        update = moments(weight, one, two, grad, 0.0)[2]
+        tile_sums[row : row + n, 0:lanes] = weight * weight * share_of
+        tile_sums[16 + row : 16 + row + n, 0:lanes] = update * update * share_of
+
     reduce.finish()
-    swap.wait_recv()
-    widen(grad_far, stream)
-    outs += [
-        pltpu.make_async_copy(stream.at[pl.ds(p * length, length)], grad_input.at[packs * (1 - x) + p], local.at[packs + p])
-        for p in range(packs)
-    ]
-    for copy in outs[packs:]:
-        copy.start()
+    for k in range(2):
+        for row in range(6):
+            tile_sums[16 * k + row : 16 * k + row + 1] = jnp.sum(squares[k, row], 0, keepdims=True)
+    every = SumSoon(place, wire, tile_sums, plane, line).value
+    norms[...] = jnp.broadcast_to(jnp.sqrt(jnp.sum(every, -1, keepdims=True)), norms.shape)
+    arrive(swaps)
     for copy in outs:
         copy.wait()
     wire.close()
 
 
-def block_step(depth, tokens, segment, pairing, images, qkv_weight, out_weight, up_weight, down_weight, affine, head_bias, inner_bias):
+def block_step(depth, *arrays):
+    tokens, segment, pairing, images, qkv_weight, out_weight, up_weight, down_weight = arrays[:8]
     packs, length, width = tokens.shape
     rows = packs // 2 * length
     share, half = qkv_weight.shape[1:]
@@ -752,64 +881,114 @@
     units = 4 + 2 * blocks
     slots = pairing.shape[1]
     h = depth // 2
-    few = images.shape[0] // 2
+    few = images.shape[0]
     ring = 4
     small = (16, width)
     low = lambda *shape: pltpu.VMEM(shape, bf16)
     wide = lambda *shape: pltpu.VMEM(shape, f32)
-    count = (units + 1) * (depth - 1 + 5) + units * (5 + depth - 1) + 2 * (3 + depth - 1) + 1
+    count = units * (depth - 1 + 5) + (depth - 1 + 2) + units * (5 + depth - 1) + 2 * (3 + depth - 1) + 2 + 7 + depth - 1
     vmem = pl.BlockSpec(memory_space=pltpu.VMEM)
     hbm = pl.BlockSpec(memory_space=pl.ANY)
     return pl.pallas_call(
         functools.partial(block_kernel, depth),
         out_shape=(
             jax.ShapeDtypeStruct((units, share, half), f32),
-            jax.ShapeDtypeStruct(small, f32),
-            jax.ShapeDtypeStruct(tokens.shape, f32),
+            jax.ShapeDtypeStruct((16, 128), f32),
+            jax.ShapeDtypeStruct((32, 128), f32),
+            jax.ShapeDtypeStruct(tokens.shape, bf16),
         ),
-        in_specs=[hbm] + [vmem] * 10,
-        out_specs=[vmem, vmem, hbm],
+        in_specs=[hbm] + [vmem] * 10 + [hbm] * 8 + [vmem] * 6,
+        out_specs=[vmem, vmem, vmem, hbm],
         scratch_shapes=[
-            low(units, depth, 2, 2, share, width), low(depth, 2, 2, 2, few, width),
+            low(units, depth, 2, 2, share, width), low(depth, 2, 2, few, width),
             low(units, depth, 2, 2, share, width), low(ring, depth, 2, share, width), low(units, h, 2, share, half),
             low(units, depth - h, share, width), low(units, h, share, half), low(units, depth - h, share, half),
             low(depth - 1, units, share, half),
             low(rows, width), low(rows, width), low(3, rows, width), low(rows, width), wide(rows, width), low(rows, width),
             low(blocks, rows, width), low(blocks, rows, width), wide(rows, width), low(rows, width), wide(rows, width), low(rows, width),
-            low(2, width // (2 * HD), length // 64, 128, 128), wide(2, length // 64, 128, 128), wide(*small),
-            wide(3 + depth, *small), wide(3 + depth, *small), wide(9, 8, width), wide(2 * slots, width), wide(length, 2 * HD), wide(length, 2 * HD),
-            low(rows, width), low(rows, width),
-            pltpu.SemaphoreType.DMA((count,)), pltpu.SemaphoreType.DMA((count,)), pltpu.SemaphoreType.REGULAR, pltpu.SemaphoreType.DMA((4,)),
+            low(2, width // (2 * HD), length // 64, 128, 128), wide(2, length // 64, 128, 128), wide(*small), wide(*small),
+            wide(3 + depth, *small), wide(3 + depth, *small), wide(9, 8, width), wide(2 * slots, width),
+            wide(2, *qkv_weight.shape), wide(2, *out_weight.shape), wide(2, *up_weight.shape), wide(2, *down_weight.shape),
+            wide(2, 6, 8, 128), wide(32, 128), wide(8, 32, 128), wide(depth, 32, 128),
+            pltpu.SemaphoreType.DMA((count,)), pltpu.SemaphoreType.DMA((count,)), pltpu.SemaphoreType.REGULAR,
+            pltpu.SemaphoreType.DMA((2,)), pltpu.SemaphoreType.DMA((8,)),
         ],
         compiler_params=pltpu.CompilerParams(collective_id=1, has_side_effects=True, vmem_limit_bytes=64 << 20),
         name="train_block",
-    )(
-        tokens, segment.reshape(packs, 1, length), pairing.reshape(packs, 1, slots), images,
-        qkv_weight, out_weight, up_weight, down_weight, affine, head_bias, inner_bias.reshape(1, -1),
-    )
-
-
-def sum_kernel(depth, own_ref, sum_ref, room, send, recv):
-    place = Place(depth)
-    place.barrier()
-    sum_ref[...] = own_ref[...]
-    SumAll(place, Wire(send, recv), sum_ref, room).run()
-
-
-def sum_all(depth, own):
+    )(*arrays)
+
+
+def finish_kernel(slot_total, total, small_grad, norms, grad_low, *refs):
+    weights, firsts, seconds = refs[0:7], refs[7:14], refs[14:21]
+    grad_input = refs[21]
+    nexts, first_nexts, second_nexts = refs[22:29], refs[29:36], refs[36:43]
+    mean_loss, tensor_norms, room, wide_room, sems = refs[43:48]
+    packs = grad_low.shape[0]
+    reads = [pltpu.make_async_copy(grad_low.at[p], room.at[p], sems.at[p]) for p in range(packs)]
+    writes = [pltpu.make_async_copy(wide_room.at[p], grad_input.at[p], sems.at[packs + p]) for p in range(packs)]
+    for copy in reads:
+        copy.start()
+
+    def update(i, at, grad, row, decay):
+        weight, one, two = weights[i][at], firsts[i][at], seconds[i][at]
+        first_new, second_new, change = moments(weight, one, two, grad, decay)
+        first_nexts[i][at] = first_new
+        second_nexts[i][at] = second_new
+        count = 1 if isinstance(row, int) else row[1]
+        row = row if isinstance(row, int) else row[0]
+        weight_norm, update_norm = norms[row : row + count, 0:1], norms[16 + row : 16 + row + count, 0:1]
+        nexts[i][at] = weight - learning_rate * weight_norm / update_norm * change
+
+    every = slice(None)
+    half = total.shape[2]
+    blocks = weights[2].shape[1] // half
+    for p in range(packs):
+        reads[p].wait()
+
+        def widen(r, p=p):
+            wide_room[p, r] = room[p, r].astype(f32)
+
+        row_loop(room.shape[1], 32, widen)
+        writes[p].start()
+    for k in range(3):
+        update(0, (k,), total[k], k, weight_decay)
+    update(1, (every,), total[3], 3, weight_decay)
+    for i in range(2):
+        for j in range(blocks):
+            update(2 + i, (every, slice(j * half, (j + 1) * half)), total[4 + i * blocks + j], 4 + i, weight_decay)
+    update(4, (every,), small_grad[0:6, 0 : weights[4].shape[1]], (6, 6), 0.0)
+    update(5, (every,), small_grad[6:8, 0 : weights[5].shape[1]], (12, 2), 0.0)
+    update(6, (every,), small_grad[8:9, 0 : weights[6].shape[1]], 14, 0.0)
+    mean_loss[...] = small_grad[9:10, 0:1] / slot_total
+    square = norms.shape[0] // 2
+    diagonal = lax.broadcasted_iota(jnp.int32, (square, square), 0) == lax.broadcasted_iota(jnp.int32, (square, square), 1)
+    for k in range(2):
+        column = jnp.broadcast_to(norms[square * k : square * (k + 1), 0:1], (square, square))
+        tensor_norms[k : k + 1] = jnp.sum(jnp.where(diagonal, column, 0.0), 0, keepdims=True)[:, 0:15]
+    for copy in writes:
+        copy.wait()
+
+
+def finish_step(slot_total, total, small_grad, norms, grad_low, weights, firsts, seconds):
     vmem = pl.BlockSpec(memory_space=pltpu.VMEM)
+    hbm = pl.BlockSpec(memory_space=pl.ANY)
+    packs, length, width = grad_low.shape
+    like = [jax.ShapeDtypeStruct(a.shape, f32) for a in weights]
     return pl.pallas_call(
-        functools.partial(sum_kernel, depth),
-        out_shape=jax.ShapeDtypeStruct(own.shape, f32),
-        in_specs=[vmem],
-        out_specs=vmem,
+        functools.partial(finish_kernel, slot_total),
+        out_shape=(
+            jax.ShapeDtypeStruct(grad_low.shape, f32), *like, *like, *like,
+            jax.ShapeDtypeStruct((1, 1), f32), jax.ShapeDtypeStruct((2, 15), f32),
+        ),
+        in_specs=[vmem] * 3 + [hbm] + [vmem] * 21,
+        out_specs=[hbm] + [vmem] * 23,
         scratch_shapes=[
-            pltpu.VMEM((3 + depth,) + own.shape, f32),
-            pltpu.SemaphoreType.DMA((3 + depth - 1,)), pltpu.SemaphoreType.DMA((3 + depth - 1,)),
+            pltpu.VMEM((packs, length, width), bf16), pltpu.VMEM((packs, length, width), f32),
+            pltpu.SemaphoreType.DMA((2 * packs,)),
         ],
-        compiler_params=pltpu.CompilerParams(collective_id=2, has_side_effects=True),
-        name="sum_squares",
-    )(own)
+        compiler_params=pltpu.CompilerParams(vmem_limit_bytes=64 << 20),
+        name="optimizer",
+    )(total, small_grad, norms, grad_low, *weights, *firsts, *seconds)
 
 
 def body_near(depth, *arrays):
@@ -820,45 +999,22 @@
         affine, affine_first, affine_second, head_bias, head_first, head_second,
         inner_bias, inner_first, inner_second,
     ) = arrays
-    mp = lax.axis_index("mp")
-    dp = lax.axis_index("dp")
-    width = tokens.shape[-1]
-    share, half = qkv_weight.shape[1:]
-    blocks = up_weight.shape[1] // half
-    dp_size = 4 * depth
-    total, sums, grad_input = block_step(
-        depth, tokens, segment, pairing, images, qkv_weight, out_weight, up_weight, down_weight, affine, head_bias, inner_bias
-    )
-
-    def uncut(a):
-        return a.transpose(1, 0, 2).reshape(share, -1)
-
-    def lane(a, at, n):
-        return lax.dynamic_slice_in_dim(a, at * n, n, a.ndim - 1)
-
-    inner_rows = 2 * blocks * half // width
-    owner = mp * dp_size + dp
-    grads = (
-        total[0:3], total[3], uncut(total[4 : 4 + blocks]), uncut(total[4 + blocks :]),
-        lane(sums[0:6], dp, affine.shape[1]),
-        lane(sums[6:8], owner, head_bias.shape[1]),
-        lane(sums[8 : 8 + inner_rows].reshape(-1), owner, inner_bias.shape[0]),
-    )
-    mean_loss = sums[8 + inner_rows, 0] / float(pairing.size * dp_size)
+    inner_bias, inner_first, inner_second = (a.reshape(1, -1) for a in (inner_bias, inner_first, inner_second))
+    total, small_grad, norms, grad_low = block_step(
+        depth, tokens, segment, pairing, images, qkv_weight, out_weight, up_weight, down_weight, affine, head_bias, inner_bias,
+        qkv_first, qkv_second, out_first, out_second, up_first, up_second, down_first, down_second,
+        affine_first, affine_second, head_first, head_second, inner_first, inner_second,
+    )
     weights = (qkv_weight, out_weight, up_weight, down_weight, affine, head_bias, inner_bias)
     firsts = (qkv_first, out_first, up_first, down_first, affine_first, head_first, inner_first)
     seconds = (qkv_second, out_second, up_second, down_second, affine_second, head_second, inner_second)
-    decays = (weight_decay, weight_decay, weight_decay, weight_decay, 0.0, 0.0, 0.0)
-    steps = [moments(weights[i], firsts[i], seconds[i], grads[i], decays[i]) for i in range(7)]
-    updates = [s[2] for s in steps]
-    squares = jnp.stack([tensor_squares(*weights, 2.0), tensor_squares(*updates, 2.0)])
-    squares = sum_all(depth, jnp.pad(squares, ((0, 6), (0, 113))))
-    norms = jnp.sqrt(squares[0:2, 0:15])
-    weight_split, update_split = split_norms(norms[0]), split_norms(norms[1])
-    results = [mean_loss, grad_input]
+    slot_total = float(pairing.size * 4 * depth)
+    grad_input, *news, mean_loss, tensor_norms = finish_step(slot_total, total, small_grad, norms, grad_low, weights, firsts, seconds)
+    results = [mean_loss.reshape(()), grad_input]
     for i in range(7):
-        results += [scaled_step(weights[i], updates[i], weight_split[i], update_split[i]), steps[i][0], steps[i][1]]
-    return (*results, norms)
+        triple = (news[i], news[7 + i], news[14 + i])
+        results += [a.reshape(-1) for a in triple] if i == 6 else triple
+    return (*results, tensor_norms)
 
 
 def body(

time: 278 us -> 234 us (0.84)
  other arithmetic: 23.8 us -> 0 us
  local copies, waits for them, and re-layouts: 14.8 us -> 0 us
  between operations: 7.91 us -> 0.85 us
    reduce_sum x6 -> x0, other arithmetic: 11.8 us -> none  [the longest x1 2.71 us: tensor_squares(): jnp.sum(qkv * qkv, (1, 2))]
    sub x7 -> x0, other arithmetic: 10.7 us -> none  [scaled_step(): return weight - learning_rate * weight_norm / update_norm * update]
    pallas_call x1, Pallas kernels: 218 us -> 227 us  [block_step(): pl.pallas_call(functools.partial(block_kernel, depth), out_shape=(jax.Sha...]
    pallas_call x1, Pallas kernels: 13.2 us -> 6.56 us  [finish_step(): pl.pallas_call(functools.partial(finish_kernel, slot_total), out_shape=(j...]
    concatenate x2 -> x0, local copies, waits for them, and re-layouts: 6.52 us -> none  [tensor_squares(): jnp.concatenate([jnp.sum(qkv * qkv, (1, 2)), jnp.sum(out * out)[None], jn...]
    slice x5 -> x0, local copies, waits for them, and re-layouts: 3.4 us -> none  [the longest x1 1.31 us: body_near(): mean_loss = sums[8 + inner_rows, 0] / float(pairing.size * dp_size)]
    unnamed x34 -> x0, local copies, waits for them, and re-layouts: 2.84 us -> none
where the time goes in v2:
time: 234 us
  Pallas kernels  233 us (100%)
    pallas_call x1, Pallas kernels, block_step(): pl.pallas_call(functools.partial(block_kernel, depth), out_shape=(jax.Sha...  227 us
    pallas_call x1, Pallas kernels, finish_step(): pl.pallas_call(functools.partial(finish_kernel, slot_total), out_shape=(j...  6.56 us

profile of v2, /device:TPU:0, one launch (start us, length us, event | category | flops | bytes accessed | tf_op | source)
XLA Modules:
  0.0 234.2 jit_solution(17624937245129806542)
XLA Ops:
  0.7 226.8 %train_block.1 = (f32[12,48,384]{2,1,0:T(8,128)}, f32[16,128]{1,0:T(8,128)}, f32[32,128]{1,0:T(8,128)}, bf16[4,256,768]{2,1,0:T(8,128)(2,1)}) custom-call(bf16[4,256,768]{2,1,0:T(8,128)(2,1)} %tokens.1, s32[4,256]{1,0:T(4,128)} %segment.1, s32[4,64]{1,0:T(4,128)} %pairing.1, bf16[64,768]{1,0:T(8,128)(2,1)} %images.1, f32[3,48,384]{2,1,0:T(8,128)} %refs_0_.1, ...), custom_call_target="tpu_custom_call" | custom-call | tf_op jit(solution)/shard_map/train_block/pallas_call | solution.py:892
  227.5 6.6 %optimizer.1 = (f32[4,256,768]{2,1,0:T(8,128)}, f32[3,48,384]{2,1,0:T(8,128)}, f32[48,384]{1,0:T(8,128)}, f32[48,1536]{1,0:T(8,128)}, f32[48,1536]{1,0:T(8,128)}...) custom-call(f32[12,48,384]{2,1,0:T(8,128)} %get-tuple-element.52.tot, ...), custom_call_target="tpu_custom_call" | custom-call | tf_op jit(solution)/shard_map/optimizer/pallas_call | solution.py:977
